TPU v7x, 32 devices: a whole 2x2x4 slice. The times are simulated.
32 devices in a mesh: dp: 16 (over z, x, core), blk: 2 (over y).
Axes of the slice: x: 2, y: 2, z: 4, core: 2. Of those that a mesh axis runs over, the one named last changes fastest.
Arguments:
- tokens: bfloat16 [2, 16, 1024, 768], P(None, 'dp', 'blk'), may hold values from -6 to 6
- segment_ids: int32 [2, 16, 1024], P(None, 'dp'), may hold values from 0 to 1022, as said below
- padding_mask: int32 [2, 16, 1024], P(None, 'dp'), may hold values from 0 to 1, as said below
- qkv_weight: bfloat16 [768, 2304], P('dp'), may hold values from -0.21875 to 0.21875
- proj_weight: bfloat16 [768, 768], P('dp'), may hold values from -0.875 to 0.875
- up_weight: bfloat16 [768, 3072], P('dp'), may hold values from -0.21875 to 0.21875
- down_weight: bfloat16 [3072, 768], P('dp'), may hold values from -0.109375 to 0.109375
- norm_gain: bfloat16 [2, 768], P(None, 'dp'), may hold values from 0.25 to 1.75
- norm_shift: bfloat16 [2, 768], P(None, 'dp'), may hold values from -4 to 4
- qv_bias: bfloat16 [2, 768], P(None, 'dp'), may hold values from -4 to 4
- out_bias: bfloat16 [2, 768], P(None, 'dp'), may hold values from -4 to 4
- up_bias: bfloat16 [3072], P('dp'), may hold values from -6 to 6
- cotangent: bfloat16 [2, 16, 1024, 768], P(None, 'dp', 'blk'), may hold values from -6 to 6
Outputs:
- layer_out: bfloat16 [2, 16, 1024, 768], P(None, 'dp', 'blk')
- grad_tokens: bfloat16 [2, 16, 1024, 768], P(None, 'dp', 'blk')
- grad_qkv: float32 [768, 2304], P('dp')
- grad_proj: float32 [768, 768], P('dp')
- grad_up: float32 [768, 3072], P('dp')
- grad_down: float32 [3072, 768], P('dp')
- grad_gain: float32 [2, 768], P(None, 'dp')
- grad_shift: float32 [2, 768], P(None, 'dp')
- grad_qv_bias: float32 [2, 768], P(None, 'dp')
- grad_out_bias: float32 [2, 768], P(None, 'dp')
- grad_up_bias: float32 [3072], P('dp')
Inputs may be any that keep to these rules, and one draw needn't show every extreme that they name: `padding_mask`: in each row the ones form a prefix of at least 768 positions; the first row of the first micro-batch has no padding. `segment_ids`: the ids of a row are 0 at position 0 and rise by 0 or 1 from one position to the next; a rise happens only at a position whose padding_mask is 1 and never at position 512; padded positions keep the row's last id. In the first row of the first micro-batch the id rises at every position where a rise may happen.
All inputs are finite; a program needn't handle non-finite values.
Results may differ from a plain program's by a relative error of at most 0.012.
Values may be sent and summed in bfloat16 or wider, within the bound.
No kernel may reach another device: no remote copies, remote signals or barrier semaphores. Data moves between devices by JAX's collectives and lax.ppermute only.
A program may use at most 256 MiB of HBM per device.

v0:
```python
import jax
import jax.numpy as jnp
from jax import lax
from jax.sharding import PartitionSpec as P

HD = 64


def layer_norm(source, gain_row, shift_row):
    center = source - jnp.mean(source, axis=-1, keepdims=True)
    spread = jnp.mean(center * center, axis=-1, keepdims=True)
    return center * lax.rsqrt(spread + 1e-05) * gain_row + shift_row


def gelu_exact(pre_act):
    return jax.nn.gelu(pre_act, approximate=False)


def contract_rows(first_mat, second_mat):
    return lax.dot_general(
        first_mat, second_mat, (((0,), (0,)), ((), ())), preferred_element_type=jnp.float32
    )


def contract_cols(first_mat, second_mat):
    return lax.dot_general(
        first_mat, second_mat, (((1,), (1,)), ((), ())), preferred_element_type=jnp.float32
    )


def fetch_weights(
    qkv_weight,
    proj_weight,
    up_weight,
    down_weight,
    norm_gain,
    norm_shift,
    qv_bias,
    out_bias,
    up_bias,
):
    return (
        lax.all_gather(qkv_weight, "dp", axis=0, tiled=True),
        lax.all_gather(proj_weight, "dp", axis=0, tiled=True),
        lax.all_gather(up_weight, "dp", axis=0, tiled=True),
        lax.all_gather(down_weight, "dp", axis=0, tiled=True),
        lax.all_gather(norm_gain, "dp", axis=1, tiled=True),
        lax.all_gather(norm_shift, "dp", axis=1, tiled=True),
        lax.all_gather(qv_bias, "dp", axis=1, tiled=True),
        lax.all_gather(out_bias, "dp", axis=1, tiled=True),
        lax.all_gather(up_bias, "dp", axis=0, tiled=True),
    )


def reduce_owned(terms):
    return (
        lax.psum_scatter(terms[0], "dp", scatter_dimension=0, tiled=True),
        lax.psum_scatter(terms[1], "dp", scatter_dimension=0, tiled=True),
        lax.psum_scatter(terms[2], "dp", scatter_dimension=0, tiled=True),
        lax.psum_scatter(terms[3], "dp", scatter_dimension=0, tiled=True),
        lax.psum_scatter(terms[4], "dp", scatter_dimension=1, tiled=True),
        lax.psum_scatter(terms[5], "dp", scatter_dimension=1, tiled=True),
        lax.psum_scatter(terms[6], "dp", scatter_dimension=1, tiled=True),
        lax.psum_scatter(terms[7], "dp", scatter_dimension=1, tiled=True),
        lax.psum_scatter(terms[8], "dp", scatter_dimension=0, tiled=True),
    )


def run_micro(gathered, tok_block, seg_block, pad_block, cot_block):
    qkv_w, proj_w, up_w, down_w, gains, shifts, qv_b, out_b, up_b = gathered
    gains_f = gains.astype(jnp.float32)
    shifts_f = shifts.astype(jnp.float32)
    row_count, half_len, model_width = tok_block.shape
    head_count = model_width // HD
    tok_count = row_count * half_len
    full_len = seg_block.shape[1]
    row_offset = lax.axis_index("blk") * half_len
    tok_flat = tok_block.astype(jnp.float32).reshape(tok_count, model_width)
    norm_in = layer_norm(tok_flat, gains_f[0], shifts_f[0]).astype(jnp.bfloat16)
    joined = jnp.dot(norm_in, qkv_w, preferred_element_type=jnp.float32)
    queries = (joined[:, :model_width] + qv_b[0]).astype(jnp.bfloat16)
    key_own = joined[:, model_width : 2 * model_width].astype(jnp.bfloat16)
    value_own = (joined[:, 2 * model_width :] + qv_b[1]).astype(jnp.bfloat16)
    key_rows, value_rows = (
        lax.all_gather(
            key_own.reshape(row_count, half_len, model_width), "blk", axis=1, tiled=True
        ),
        lax.all_gather(
            value_own.reshape(row_count, half_len, model_width), "blk", axis=1, tiled=True
        ),
    )
    query_lead = jnp.transpose(queries.reshape(row_count, half_len, head_count, HD), (2, 0, 1, 3))
    key_lead = jnp.transpose(key_rows.reshape(row_count, full_len, head_count, HD), (2, 0, 1, 3))
    value_lead = jnp.transpose(
        value_rows.reshape(row_count, full_len, head_count, HD), (2, 0, 1, 3)
    )
    own_seg = lax.dynamic_slice_in_dim(seg_block, row_offset, half_len, 1)
    allowed = (own_seg[:, :, None] == seg_block[:, None, :]) & (pad_block[:, None, :] == 1)

    def masked_scores(query_one, key_one):
        raw_scores = (
            jnp.einsum("rqd,rkd->rqk", query_one, key_one, preferred_element_type=jnp.float32)
            * 0.125
        )
        return jnp.where(allowed, raw_scores, -1e30)

    def head_forward(operands):
        query_one, key_one, value_one = operands
        scores = masked_scores(query_one, key_one)
        row_top = jnp.max(scores, axis=-1, keepdims=True)
        exp_scores = jnp.exp(scores - row_top)
        norm_sum = jnp.sum(exp_scores, axis=-1, keepdims=True)
        probs_low = (exp_scores / norm_sum).astype(jnp.bfloat16)
        attended_one = jnp.einsum(
            "rqk,rkd->rqd", probs_low, value_one, preferred_element_type=jnp.float32
        )
        return (attended_one, row_top, norm_sum)

    attended_lead, top_lead, sum_lead = lax.map(head_forward, (query_lead, key_lead, value_lead))
    attended = (
        jnp.transpose(attended_lead, (1, 2, 0, 3))
        .reshape(tok_count, model_width)
        .astype(jnp.bfloat16)
    )
    residual_mid = (
        tok_flat + jnp.dot(attended, proj_w, preferred_element_type=jnp.float32) + out_b[0]
    )
    norm_mid = layer_norm(residual_mid, gains_f[1], shifts_f[1]).astype(jnp.bfloat16)
    pre_act = jnp.dot(norm_mid, up_w, preferred_element_type=jnp.float32) + up_b
    act_full, gelu_pull = jax.vjp(gelu_exact, pre_act)
    act_low = act_full.astype(jnp.bfloat16)
    block_out = (
        residual_mid + jnp.dot(act_low, down_w, preferred_element_type=jnp.float32) + out_b[1]
    )
    cot_low = cot_block.reshape(tok_count, model_width)
    cot_full = cot_low.astype(jnp.float32)
    grad_down = contract_rows(act_low, cot_low)
    grad_bdown = jnp.sum(cot_full, axis=0)
    d_pre = gelu_pull(contract_cols(cot_low, down_w))[0].astype(jnp.bfloat16)
    grad_up = contract_rows(norm_mid, d_pre)
    grad_bup = jnp.sum(d_pre.astype(jnp.float32), axis=0)
    unused_mid, mid_pull = jax.vjp(layer_norm, residual_mid, gains_f[1], shifts_f[1])
    d_mid_norm, grad_gain_mid, grad_shift_mid = mid_pull(contract_cols(d_pre, up_w))
    d_mid = cot_full + d_mid_norm
    d_branch = d_mid.astype(jnp.bfloat16)
    grad_proj = contract_rows(attended, d_branch)
    grad_bout = jnp.sum(d_branch.astype(jnp.float32), axis=0)
    d_attended = (
        contract_cols(d_branch, proj_w)
        .astype(jnp.bfloat16)
        .reshape(row_count, half_len, head_count, HD)
    )
    d_att_lead = jnp.transpose(d_attended, (2, 0, 1, 3))

    def head_backward(operands):
        query_one, key_one, value_one, d_att_one, top_one, sum_one = operands
        scores = masked_scores(query_one, key_one)
        probs_low = (jnp.exp(scores - top_one) / sum_one).astype(jnp.bfloat16)
        attn_probs = jnp.exp(scores - (top_one + jnp.log(sum_one)))
        d_probs = jnp.einsum(
            "rqd,rkd->rqk", d_att_one, value_one, preferred_element_type=jnp.float32
        )
        inner_sum = jnp.sum(attn_probs * d_probs, axis=-1, keepdims=True)
        d_scores = (attn_probs * (d_probs - inner_sum)).astype(jnp.bfloat16)
        d_query_one = (
            jnp.einsum("rqk,rkd->rqd", d_scores, key_one, preferred_element_type=jnp.float32)
            * 0.125
        )
        key_term_one = (
            jnp.einsum("rqk,rqd->rkd", d_scores, query_one, preferred_element_type=jnp.float32)
            * 0.125
        )
        value_term_one = jnp.einsum(
            "rqk,rqd->rkd", probs_low, d_att_one, preferred_element_type=jnp.float32
        )
        return (d_query_one, key_term_one, value_term_one)

    dq_lead, key_lead_terms, value_lead_terms = lax.map(
        head_backward, (query_lead, key_lead, value_lead, d_att_lead, top_lead, sum_lead)
    )
    d_query = (
        jnp.transpose(dq_lead, (1, 2, 0, 3)).reshape(tok_count, model_width).astype(jnp.bfloat16)
    )
    key_terms = jnp.transpose(key_lead_terms, (1, 2, 0, 3)).reshape(
        row_count, full_len, model_width
    )
    value_terms = jnp.transpose(value_lead_terms, (1, 2, 0, 3)).reshape(
        row_count, full_len, model_width
    )
    d_keys, d_values = (
        lax.psum_scatter(
            key_terms.astype(jnp.bfloat16), "blk", scatter_dimension=1, tiled=True
        ).astype(jnp.float32),
        lax.psum_scatter(
            value_terms.astype(jnp.bfloat16), "blk", scatter_dimension=1, tiled=True
        ).astype(jnp.float32),
    )
    d_keys = d_keys.reshape(tok_count, model_width).astype(jnp.bfloat16)
    d_values = d_values.reshape(tok_count, model_width).astype(jnp.bfloat16)
    d_joined = jnp.concatenate([d_query, d_keys, d_values], axis=1)
    grad_qkv = contract_rows(norm_in, d_joined)
    grad_bq = jnp.sum(d_query.astype(jnp.float32), axis=0)
    grad_bv = jnp.sum(d_values.astype(jnp.float32), axis=0)
    unused_in, in_pull = jax.vjp(layer_norm, tok_flat, gains_f[0], shifts_f[0])
    d_tok_norm, grad_gain_in, grad_shift_in = in_pull(contract_cols(d_joined, qkv_w))
    d_tokens = d_mid + d_tok_norm
    gradients = (
        grad_qkv,
        grad_proj,
        grad_up,
        grad_down,
        jnp.stack([grad_gain_in, grad_gain_mid]),
        jnp.stack([grad_shift_in, grad_shift_mid]),
        jnp.stack([grad_bq, grad_bv]),
        jnp.stack([grad_bout, grad_bdown]),
        grad_bup,
    )
    layer_piece = block_out.astype(jnp.bfloat16).reshape(row_count, half_len, model_width)
    grad_piece = d_tokens.astype(jnp.bfloat16).reshape(row_count, half_len, model_width)
    return (layer_piece, grad_piece, gradients)


def shards(
    tokens,
    segment_ids,
    padding_mask,
    qkv_weight,
    proj_weight,
    up_weight,
    down_weight,
    norm_gain,
    norm_shift,
    qv_bias,
    out_bias,
    up_bias,
    cotangent,
):
    micro_count = tokens.shape[0]
    running = None
    out_list = []
    grad_list = []
    for which_micro in range(micro_count):
        gathered = fetch_weights(
            qkv_weight,
            proj_weight,
            up_weight,
            down_weight,
            norm_gain,
            norm_shift,
            qv_bias,
            out_bias,
            up_bias,
        )
        layer_piece, grad_piece, gradients = run_micro(
            gathered,
            tokens[which_micro],
            segment_ids[which_micro],
            padding_mask[which_micro],
            cotangent[which_micro],
        )
        out_list.append(layer_piece)
        grad_list.append(grad_piece)
        running = gradients if running is None else jax.tree.map(jnp.add, running, gradients)
    owned_sums = reduce_owned(running)
    final = (
        lax.psum(owned_sums[0].astype(jnp.bfloat16), "blk").astype(jnp.float32),
        lax.psum(owned_sums[1].astype(jnp.bfloat16), "blk").astype(jnp.float32),
        lax.psum(owned_sums[2].astype(jnp.bfloat16), "blk").astype(jnp.float32),
        lax.psum(owned_sums[3].astype(jnp.bfloat16), "blk").astype(jnp.float32),
        lax.psum(owned_sums[4].astype(jnp.bfloat16), "blk").astype(jnp.float32),
        lax.psum(owned_sums[5].astype(jnp.bfloat16), "blk").astype(jnp.float32),
        lax.psum(owned_sums[6].astype(jnp.bfloat16), "blk").astype(jnp.float32),
        lax.psum(owned_sums[7].astype(jnp.bfloat16), "blk").astype(jnp.float32),
        lax.psum(owned_sums[8].astype(jnp.bfloat16), "blk").astype(jnp.float32),
    )
    layer_out = jnp.stack(out_list)
    grad_tokens = jnp.stack(grad_list)
    return (
        layer_out,
        grad_tokens,
        final[0],
        final[1],
        final[2],
        final[3],
        final[4],
        final[5],
        final[6],
        final[7],
        final[8],
    )


def solution(mesh):
    return jax.shard_map(
        shards,
        mesh=mesh,
        in_specs=(
            P(None, "dp", "blk", None),
            P(None, "dp", None),
            P(None, "dp", None),
            P("dp", None),
            P("dp", None),
            P("dp", None),
            P("dp", None),
            P(None, "dp"),
            P(None, "dp"),
            P(None, "dp"),
            P(None, "dp"),
            P("dp"),
            P(None, "dp", "blk", None),
        ),
        out_specs=(
            P(None, "dp", "blk", None),
            P(None, "dp", "blk", None),
            P("dp", None),
            P("dp", None),
            P("dp", None),
            P("dp", None),
            P(None, "dp"),
            P(None, "dp"),
            P(None, "dp"),
            P(None, "dp"),
            P("dp"),
        ),
        check_vma=False,
    )
```

profile of v0, /device:TPU:0, one launch (start us, length us, event | category | flops | bytes accessed | tf_op | source)
XLA Modules:
  0.0 1354.3 jit_solution(4937723924767434913)
XLA Ops:
  8.0 23.1 %all-gather.4 = bf16[16,48,2]{1,2,0:T(2,128)(2,1)S(1)} all-gather(bf16[1,48,2]{1,2,0:T(2,128)(2,1)} %bitcast.496), channel_id=1, replica_groups=mesh['dp'=16,'blk'=2] {'dp'}, dimensions={0}, use_global_device_ids=true | all-gather | bytes 3264 | tf_op jit(solution)/shard_map/all_gather | solution.py:47
  31.2 17.5 %all-gather.5 = bf16[16,48,2]{1,2,0:T(2,128)(2,1)S(1)} all-gather(bf16[1,48,2]{1,2,0:T(2,128)(2,1)} %bitcast.497), channel_id=1, replica_groups=mesh['dp'=16,'blk'=2] {'dp'}, dimensions={0}, use_global_device_ids=true | all-gather | bytes 3264 | tf_op jit(solution)/shard_map/all_gather | solution.py:48
  48.8 18.9 %all-gather.6 = bf16[16,48,2]{1,2,0:T(2,128)(2,1)S(1)} all-gather(bf16[1,48,2]{1,2,0:T(2,128)(2,1)} %bitcast.498), channel_id=1, replica_groups=mesh['dp'=16,'blk'=2] {'dp'}, dimensions={0}, use_global_device_ids=true | all-gather | bytes 3264 | tf_op jit(solution)/shard_map/all_gather | solution.py:49
  88.3 17.3 %all-gather.7 = bf16[16,48,2]{1,2,0:T(2,128)(2,1)S(1)} all-gather(bf16[1,48,2]{1,2,0:T(2,128)(2,1)S(1)} %bitcast.499), channel_id=1, replica_groups=mesh['dp'=16,'blk'=2] {'dp'}, dimensions={0}, use_global_device_ids=true | all-gather | bytes 3264 | tf_op jit(solution)/shard_map/all_gather | solution.py:50
  107.9 32.1 %all-reduce = bf16[3072]{0:T(1024)(128)(2,1)S(1)} all-reduce(bf16[3072]{0:T(1024)(128)(2,1)S(1)} %dynamic-update-slice), channel_id=1, replica_groups=mesh['dp'=16,'blk'=2] {'dp'}, use_global_device_ids=true, to_apply=%add | all-reduce | flops 3072 | bytes 12288
  153.9 46.5 %while.60 = (s32[]{:T(128)}, bf16[12,1,512,64]{2,3,1,0:T(8,128)(2,1)S(1)}, f32[12,1,512,1]{2,3,1,0:T(1,128)S(1)}, f32[12,1,512,1]{2,3,1,0:T(1,128)S(1)}, bf16[12...) while((s32[]{:T(128)}, ...), condition=%wide.region_5.6_spmd.clone, body=%wide.region_2.5_spmd.clone.sunk | while | flops 139459584 | bytes 7105649 | solution.py:119
  208.9 21.6 %all-gather.29.cloned.1.call-done = bf16[1024,768]{1,0:T(8,128)(2,1)} async-done(((bf16[512,768]{1,0:T(8,128)(2,1)}), bf16[1024,768]{1,0:T(8,128)(2,1)}) %all-gather.29.cloned.1.call-update) | async-done | bytes 1572880 | tf_op jit(solution)/shard_map/all_gather | solution.py:85
  235.2 46.5 %while.61 = (s32[]{:T(128)}, bf16[12,1,512,64]{2,3,1,0:T(8,128)(2,1)S(1)}, f32[12,1,512,1]{2,3,1,0:T(1,128)S(1)}, f32[12,1,512,1]{2,3,1,0:T(1,128)S(1)}, bf16[12...) while((s32[]{:T(128)}, ...), condition=%wide.region_13.14_spmd.clone, body=%wide.region_10.13_spmd.clone.sunk | while | flops 139459584 | bytes 7105649 | solution.py:119
  293.8 34.9 %multiply_convert_fusion.3 = (bf16[512,3072]{1,0:T(8,128)(2,1)}, f32[512,3072]{1,0:T(8,128)}, bf16[512,3072]{1,0:T(8,128)(2,1)}, f32[512,3072]{1,0:T(8,128)}, f32[512,3072]{1,0:T(8,128)}) fusion(f32[3072]{0:T(1024)S(1)} %convert_element_type.355, f32[512,3072]{1,0:T(8,128)S(1)} %fusion.170, bf16[768,3072]{1,0:T(8,128)(2,1)S(1)} %copy-done.67, ...), kind=kOutput, calls=%fused_computation.131 | convolution fusion | flops 2625503232 | bytes 37771264 | tf_op jit(solution)/shard_map/dot_general | solution.py:129
  328.7 11.7 all-gather.23.cloned.1.call-done
  340.5 8.6 convert_reduce_fusion
  352.6 8.7 convert_reduce_fusion.1
  375.4 118.4 %while.62 = (s32[]{:T(128)}, bf16[12,1,512,64]{2,3,1,0:T(8,128)(2,1)}, bf16[12,1,1024,64]{2,3,1,0:T(8,128)(2,1)S(1)}, bf16[12,1,1024,64]{2,3,1,0:T(8,128)(2,1)},...) while((s32[]{:T(128)}, ...), condition=%wide.region_20.21_spmd.clone, body=%wide.region_18.20_spmd.clone.sunk | while | flops 342982656 | bytes 17602696 | solution.py:178
  502.9 118.8 %while.63 = (s32[]{:T(128)}, bf16[12,1,512,64]{2,3,1,0:T(8,128)(2,1)S(1)}, bf16[12,1,1024,64]{2,3,1,0:T(8,128)(2,1)}, bf16[12,1,1024,64]{2,3,1,0:T(8,128)(2,1)},...) while((s32[]{:T(128)}, ...), condition=%wide.region_29.30_spmd.clone, body=%wide.region_27.29_spmd.clone.sunk | while | flops 342982656 | bytes 17602696 | solution.py:178
  646.5 28.8 %reduce-scatter.25.cloned.1.call-done = bf16[1,512,768]{1,2,0:T(8,128)(2,1)} async-done(((bf16[1,1024,768]{1,2,0:T(8,128)(2,1)}), bf16[1,512,768]{1,2,0:T(8,128)(2,1)}) %reduce-scatter.25.cloned.1.call-update) | async-done | bytes 786448 | tf_op jit(solution)/shard_map/reduce_scatter | solution.py:191
  675.3 9.0 convolution_add_fusion
  709.7 61.8 %all-reduce.1 = bf16[3072]{0:T(1024)(128)(2,1)S(1)} all-reduce(f32[3072]{0:T(1024)S(1)} %add.345), channel_id=18, replica_groups=mesh['dp'=16,'blk'=2] {'dp'}, use_global_device_ids=true, to_apply=%region_68.69.clone | all-reduce | flops 3072 | bytes 18432
  802.7 91.4 %reduce-scatter.29.cloned.1.call-done = f32[48,2304]{1,0:T(8,128)} async-done(((f32[768,2304]{1,0:T(8,128)}), f32[48,2304]{1,0:T(8,128)}) %reduce-scatter.29.cloned.1.call-update) | async-done | bytes 442384 | tf_op jit(solution)/shard_map/reduce_scatter | solution.py:57
  895.9 113.7 %reduce-scatter.35.cloned.1.call-done = f32[192,768]{1,0:T(8,128)} async-done(((f32[3072,768]{1,0:T(8,128)}), f32[192,768]{1,0:T(8,128)}) %reduce-scatter.35.cloned.1.call-update) | async-done | bytes 589840 | tf_op jit(solution)/shard_map/reduce_scatter | solution.py:60
  1011.4 113.3 %reduce-scatter.33.cloned.1.call-done = f32[48,3072]{1,0:T(8,128)} async-done(((f32[768,3072]{1,0:T(8,128)}), f32[48,3072]{1,0:T(8,128)}) %reduce-scatter.33.cloned.1.call-update) | async-done | bytes 589840 | tf_op jit(solution)/shard_map/reduce_scatter | solution.py:59
  1131.4 52.9 %reduce-scatter.41.cloned.1.call-done = f32[48,2]{1,0:T(8,128)} async-done(((f32[768,2]{1,0:T(8,128)}), f32[48,2]{1,0:T(8,128)}) %reduce-scatter.41.cloned.1.call-update) | async-done | bytes 400
  1185.2 57.9 %reduce-scatter.39.cloned.1.call-done = f32[48,2]{1,0:T(8,128)} async-done(((f32[768,2]{1,0:T(8,128)}), f32[48,2]{1,0:T(8,128)}) %reduce-scatter.39.cloned.1.call-update) | async-done | bytes 400
  1243.9 58.1 %reduce-scatter.37.cloned.1.call-done = f32[48,2]{1,0:T(8,128)} async-done(((f32[768,2]{1,0:T(8,128)}), f32[48,2]{1,0:T(8,128)}) %reduce-scatter.37.cloned.1.call-update) | async-done | bytes 400
  1310.6 30.6 %all-reduce.6.cloned.1.call-done = (bf16[48,2304]{1,0:T(8,128)(2,1)}, bf16[48,768]{1,0:T(8,128)(2,1)}, bf16[48,3072]{1,0:T(8,128)(2,1)}, bf16[192,768]{1,0:T(8,128)(2,1)}) async-done(((bf16[48,2304]{1,0:T(8,128)(2,1)}, bf16[48,768]{1,0:T(8,128)(2,1)}, bf16[48,3072]{1,0:T(8,128)(2,1)}, bf16[192,768]{1,0:T(8,128)(2,1)}), (bf16[48,2304]{1,0:T(8,128)(2,1)}, bf16[48,768]{1,0:T(8,128)(2,1)}, ...) | async-done | bytes 884752 | tf_op jit(solution)/shard_map/psum | solution.py:266
  (632 shorter events, 524.0 us)
Async XLA Ops:
  7.2 62.4 %copy-start = (bf16[2,1,512,768]{3,2,1,0:T(8,128)(2,1)S(1)}, bf16[2,1,512,768]{3,2,1,0:T(8,128)(2,1)}, u32[]{:S(2)}) copy-start(bf16[2,1,512,768]{3,2,1,0:T(8,128)(2,1)} %param.21) | copy-start | bytes 4718596
  7.2 63.6 %all-gather.17.cloned.1.call-start = ((), (), s32[]{:S(2)}) async-start(), calls=%async_computation.12 | async-start | bytes 3760128 | tf_op jit(solution)/shard_map/all_gather | solution.py:43
  7.9 136.8 %all-gather.27.cloned.1.call-start = ((), (), s32[]{:S(2)}) async-start(), calls=%async_computation.25 | async-start | bytes 2359296 | tf_op jit(solution)/shard_map/all_gather | solution.py:88
  80.4 68.9 %all-gather.25.cloned.1.call-start = ((), (), s32[]{:S(2)}) async-start(), calls=%async_computation.24 | async-start | bytes 2359296 | tf_op jit(solution)/shard_map/all_gather | solution.py:85
  82.9 117.5 %all-gather.19.cloned.1.call-start = ((), (), s32[]{:S(2)}) async-start(), calls=%async_computation.13 | async-start | bytes 1253376 | tf_op jit(solution)/shard_map/all_gather | solution.py:44
  83.5 120.9 %all-gather.31.cloned.1.call-start = ((), (), s32[]{:S(2)}) async-start(), calls=%async_computation.27 | async-start | bytes 2359296 | tf_op jit(solution)/shard_map/all_gather | solution.py:88
  84.1 146.5 %all-gather.29.cloned.1.call-start = ((), (), s32[]{:S(2)}) async-start(), calls=%async_computation.26 | async-start | bytes 2359296 | tf_op jit(solution)/shard_map/all_gather | solution.py:85
  86.7 199.6 %all-gather.21.cloned.1.call-start = ((), (), s32[]{:S(2)}) async-start(), calls=%async_computation.14 | async-start | bytes 5013504 | tf_op jit(solution)/shard_map/all_gather | solution.py:45
  87.5 253.0 %all-gather.23.cloned.1.call-start = ((), (), s32[]{:S(2)}) async-start(), calls=%async_computation.15 | async-start | bytes 5013504 | tf_op jit(solution)/shard_map/all_gather | solution.py:46
  88.2 543.7 %reduce-scatter.23.cloned.1.call-start = ((), (), s32[]{:S(2)}) async-start(), calls=%async_computation.17 | async-start | bytes 2359296 | tf_op jit(solution)/shard_map/reduce_scatter | solution.py:194
  493.8 138.1 %reduce-scatter.21.cloned.1.call-start = ((), (), s32[]{:S(2)}) async-start(), calls=%async_computation.16 | async-start | bytes 2359296 | tf_op jit(solution)/shard_map/reduce_scatter | solution.py:191
  500.1 146.4 %reduce-scatter.27.cloned.1.call-start = ((), (), s32[]{:S(2)}) async-start(), calls=%async_computation.19 | async-start | bytes 2359296 | tf_op jit(solution)/shard_map/reduce_scatter | solution.py:194
  621.8 53.5 %reduce-scatter.25.cloned.1.call-start = ((), (), s32[]{:S(2)}) async-start(), calls=%async_computation.18 | async-start | bytes 2359296 | tf_op jit(solution)/shard_map/reduce_scatter | solution.py:191
  622.4 162.0 %reduce-scatter.43.cloned.1.call-start = ((), (), s32[]{:S(2)}) async-start(), calls=%async_computation.31 | async-start | bytes 417792
  627.1 174.1 %reduce-scatter.31.cloned.1.call-start = ((), (), s32[]{:S(2)}) async-start(), calls=%async_computation.21 | async-start | bytes 2506752 | tf_op jit(solution)/shard_map/reduce_scatter | solution.py:58
  631.3 262.8 %reduce-scatter.29.cloned.1.call-start = ((), (), s32[]{:S(2)}) async-start(), calls=%async_computation.20 | async-start | bytes 7520256 | tf_op jit(solution)/shard_map/reduce_scatter | solution.py:57
  684.3 325.2 %reduce-scatter.35.cloned.1.call-start = ((), (), s32[]{:S(2)}) async-start(), calls=%async_computation.23 | async-start | bytes 10027008 | tf_op jit(solution)/shard_map/reduce_scatter | solution.py:60
  694.8 429.9 %reduce-scatter.33.cloned.1.call-start = ((), (), s32[]{:S(2)}) async-start(), calls=%async_computation.22 | async-start | bytes 10027008 | tf_op jit(solution)/shard_map/reduce_scatter | solution.py:59
  706.1 65.4 %copy-start.55 = (f32[768]{0:T(1024)S(1)}, f32[768]{0:T(1024)}, u32[]{:S(2)}) copy-start(f32[768]{0:T(1024)} %get-tuple-element.507) | copy-start | bytes 9220
  706.1 478.2 %reduce-scatter.41.cloned.1.call-start = ((), (), s32[]{:S(2)}) async-start(), calls=%async_computation.30 | async-start | bytes 417792
  795.1 448.0 %reduce-scatter.39.cloned.1.call-start = ((), (), s32[]{:S(2)}) async-start(), calls=%async_computation.29 | async-start | bytes 417792
  799.2 502.8 %reduce-scatter.37.cloned.1.call-start = ((), (), s32[]{:S(2)}) async-start(), calls=%async_computation.28 | async-start | bytes 417792
  799.3 327.2 %copy-start.3 = (f32[512,768]{1,0:T(8,128)S(1)}, f32[512,768]{1,0:T(8,128)}, u32[]{:S(2)}) copy-start(f32[512,768]{1,0:T(8,128)} %copy-done.2) | copy-start | bytes 4718596
  800.3 540.9 %all-reduce.6.cloned.1.call-start = ((), (), s32[]{:S(2)}) async-start(), calls=%async_computation.32 | async-start | bytes 1769472 | tf_op jit(solution)/shard_map/psum | solution.py:266
  (72 other events, 424.1 us)
Sparse Core Ops, SparseCore 0:
  10.3 49.8 all-gather.16
  80.5 24.4 all-gather.26
  106.6 27.1 all-gather.24
  135.9 38.3 all-gather.18
  175.7 26.1 all-gather.30
  203.3 27.2 all-gather.28
  232.8 53.4 all-gather.20
  288.6 51.8 all-gather.22
  493.9 24.6 reduce-scatter.22
  520.7 26.0 reduce-scatter.20
  621.9 24.5 reduce-scatter.26
  649.2 26.0 reduce-scatter.24
  679.4 55.6 reduce-scatter.42
  739.2 61.9 reduce-scatter.30
  805.0 89.0 reduce-scatter.28
  898.7 110.8 reduce-scatter.34
  1013.5 111.1 reduce-scatter.32
  1129.0 55.3 reduce-scatter.40
  1188.4 54.6 reduce-scatter.38
  1247.4 54.5 reduce-scatter.36
  1305.1 36.0 all-reduce.5
where the time goes:
time: 1370 us; the launch traced here: 1350 us
  waiting for transfers between devices  593 us (43%)
  matrix products  432 us (32%)
  blocking collectives  176 us (13%)
  local copies, waits for them, and re-layouts  71.5 us (5%)
  other arithmetic  62.3 us (5%)
  between operations  17.2 us (1%)
    unnamed x25, waiting for transfers between devices  173 us
    reduce_scatter x1, waiting for transfers between devices, reduce_owned(): lax.psum_scatter(terms[3], 'dp', scatter_dimension=0, tiled=True)  114 us
    reduce_scatter x1, waiting for transfers between devices, reduce_owned(): lax.psum_scatter(terms[2], 'dp', scatter_dimension=0, tiled=True)  113 us
    unnamed x2, blocking collectives  93.9 us
    reduce_scatter x1, waiting for transfers between devices, reduce_owned(): lax.psum_scatter(terms[0], 'dp', scatter_dimension=0, tiled=True)  91.4 us
    dot_general x48, matrix products, masked_scores(): jnp.einsum('rqd,rkd->rqk', query_one, key_one, preferred_element_type=jnp...  79.8 us
    dot_general x24, matrix products, head_backward(): jnp.einsum('rqk,rqd->rkd', probs_low, d_att_one, preferred_element_type=j...  50 us
    dot_general x8, matrix products, contract_rows(): lax.dot_general(first_mat, second_mat, (((0,), (0,)), ((), ())), preferre...  45.2 us
  transfers between devices with their start and end apart: 21, of which 13 were waited for; matrix products, arithmetic and copies ran while one was open for 29% of the time, Pallas kernels for 0%

commit v1 on v0

v1 whole, which is shorter than its diff:
```python
import functools

import jax
import jax.numpy as jnp
import numpy as np
from jax import lax
from jax.experimental import pallas as pl
from jax.experimental.pallas import tpu as pltpu
from jax.sharding import PartitionSpec as P

HD = 64
BLOCKS = 16
NT = (((1,), (1,)), ((), ()))
TN = (((0,), (0,)), ((), ()))
F32 = jnp.float32
BF16 = jnp.bfloat16
ANY = pl.BlockSpec(memory_space=pl.ANY)
SMEM = pl.BlockSpec(memory_space=pltpu.SMEM)
VMEM_LIMIT = 60 << 20
MASKED = -1e30


def dot(a, b, dims=(((1,), (0,)), ((), ()))):
    return lax.dot_general(a, b, dims, preferred_element_type=F32)


def cost(us):
    return pl.CostEstimate(flops=int(us * 1.1e9), bytes_accessed=1 << 20, transcendentals=0)


def full(shape):
    return pl.BlockSpec(shape, lambda *_: (0,) * len(shape))


def params():
    return pltpu.CompilerParams(vmem_limit_bytes=VMEM_LIMIT)


def norm_stats(x):
    mean = jnp.mean(x, axis=1, keepdims=True)
    center = x - mean
    rstd = lax.rsqrt(jnp.mean(center * center, axis=1, keepdims=True) + 1e-05)
    return center * rstd, rstd


def norm_back(e, nhat, rstd):
    return (
        e - jnp.mean(e, axis=1, keepdims=True) - nhat * jnp.mean(e * nhat, axis=1, keepdims=True)
    ) * rstd


def row_sum(x):
    return jnp.sum(x, axis=0, keepdims=True)


def attn_forward_body(quad, block, idx, *refs):
    first = quad == 0
    if first:
        (own, sib, tok_own, tok_rx, sq, sk, q_o, k_o, v_o, att_o, li_o, e_o, w_o, nrm_o, small_o,
         w_s, s_s, kk, vv, aa, sem) = refs
    else:
        (own, sib, nrm_i, small_i, sq, sk, q_o, k_o, v_o, att_o, li_o, e_o, w_o,
         w_s, kk, vv, aa, sem) = refs
    seq = sq.shape[0]
    half = seq // 2
    n_part = own.shape[0]
    pair = pl.program_id(0)

    @pl.when(pair == 0)
    def _():
        copies = []
        for j, part in enumerate((own, sib)):
            for t in range(n_part):
                at = idx[j * n_part + t]
                copies.append(
                    pltpu.make_async_copy(
                        part.at[t, pl.ds(48 * quad, 48), :], w_s.at[at], sem.at[0, j * n_part + t]
                    )
                )
                if first:
                    copies.append(
                        pltpu.make_async_copy(
                            part.at[t, pl.ds(144, 16), :],
                            s_s.at[j * n_part + t],
                            sem.at[1, j * n_part + t],
                        )
                    )
        for c in copies:
            c.start()
        for c in copies:
            c.wait()
        weight = w_s[...].reshape(768, 768)
        w_o[...] = weight
        if first:
            small = jnp.zeros((16, 768), F32)
            for t in range(2 * n_part):
                small = small + s_s[t].astype(F32)
            small_o[...] = small
            gain, shift = small[0:1], small[2:3]
            for src, where in ((tok_own, idx[16]), (tok_rx, 1 - idx[16])):
                base = pl.multiple_of(where * half, half)
                for i in range(0, half, block):
                    nhat, _rstd = norm_stats(src[i : i + block, :].astype(F32))
                    nrm_o[pl.ds(base + i, block), :] = (nhat * gain + shift).astype(BF16)
            nrm = nrm_o
            bq, bv = small[4:5, 0:256], small[5:6, 0:256]
        else:
            nrm = nrm_i
            cols = slice(256 * quad, 256 * quad + 256)
            bq, bv = small_i[4:5, cols], small_i[5:6, cols]
        for i in range(0, seq, block):
            rows = slice(i, i + block)
            joined = dot(nrm[rows, :], weight)
            q_o[rows, :] = (joined[:, 0:256] + bq).astype(BF16)
            k_o[rows, :] = joined[:, 256:512].astype(BF16)
            v_o[rows, :] = (joined[:, 512:768] + bv).astype(BF16)

    lanes = pl.ds(pl.multiple_of(pair * 128, 128), 128)
    head = lax.broadcasted_iota(jnp.int32, (seq, 128), 1) // HD
    k_pair, v_pair = k_o[:, lanes], v_o[:, lanes]
    zero, one = jnp.zeros((seq, 128), BF16), jnp.ones((seq, 128), BF16)
    for h in range(2):
        mine = head == h
        kk[h, :, 0:128] = jnp.where(mine, k_pair, zero)
        kk[h, :, 128:256] = sk[...]
        vv[h, :, 0:128] = jnp.where(mine, v_pair, zero)
        vv[h, :, 128:256] = jnp.where(mine, one, zero)
    aa[:, 0:128] = q_o[:, lanes] * BF16(0.125)
    aa[:, 128:256] = sq[...]
    for i in range(0, seq, block):
        rows = slice(i, i + block)
        acc = None
        for h in range(2):
            s = dot(aa[rows, :], kk[h], NT)
            e = jnp.exp(s - jnp.max(s, axis=1, keepdims=True)).astype(BF16)
            e_o[h, rows, :] = e
            o = dot(e, vv[h])
            acc = o if acc is None else acc + o
        inverse = 1.0 / acc[:, 128:256]
        li_o[rows, :] = inverse
        att_o[rows, :] = (acc[:, 0:128] * inverse).astype(BF16)


def attn_forward(quad, idx, own, sib, rows_in, sq, sk):
    seq = sq.shape[0]
    sds = jax.ShapeDtypeStruct
    first = quad == 0
    pair_block = pl.BlockSpec((seq, 128), lambda p: (0, p))
    quad_block = full((seq, 256))
    out_shape = [
        sds((seq, 256), BF16),
        sds((seq, 256), BF16),
        sds((seq, 256), BF16),
        sds((seq, 256), BF16),
        sds((seq, 256), F32),
        sds((4, seq, seq), BF16),
        sds((768, 768), BF16),
    ]
    out_specs = [
        quad_block, quad_block, quad_block, pair_block, pair_block,
        pl.BlockSpec((2, seq, seq), lambda p: (p, 0, 0)), full((768, 768)),
    ]
    scratch = [pltpu.VMEM((BLOCKS, 48, 768), BF16)]
    if first:
        out_shape += [sds((seq, 768), BF16), sds((16, 768), F32)]
        out_specs += [full((seq, 768)), full((16, 768))]
        scratch += [pltpu.VMEM((BLOCKS, 16, 768), BF16)]
    scratch += [
        pltpu.VMEM((2, seq, 256), BF16),
        pltpu.VMEM((2, seq, 256), BF16),
        pltpu.VMEM((seq, 256), BF16),
        pltpu.SemaphoreType.DMA((2, BLOCKS)),
    ]
    return pl.pallas_call(
        functools.partial(attn_forward_body, quad, 256),
        grid=(2,),
        in_specs=[SMEM, ANY, ANY]
        + [full(r.shape) for r in rows_in]
        + [full(sq.shape), full(sk.shape)],
        out_specs=out_specs,
        out_shape=out_shape,
        scratch_shapes=scratch,
        compiler_params=params(),
        cost_estimate=cost(11),
    )(idx, own, sib, *rows_in, sq, sk)


def ffn_body(
    block, idx, gathered, att0, att1, att2, tok_own, tok_rx, cot_own, cot_rx, small,
    lo_mine, lo_theirs, dmid_o, datt_o, g_mine, g_theirs, sums_o,
    up_s, dn_s, proj_s, att_s, mid_s, nm_s, nmt_s, cot_s, act_s, dp_s, oacc, dacc, dbr_s, gbuf, gproj,
    wsem, psem, gsem, gpsem,
):
    c = pl.program_id(0)
    n_c = pl.num_programs(0)
    slot = lax.rem(c, 2)
    seq = mid_s.shape[0]
    half = seq // 2
    core = idx[17]

    def weight_copies(chunk, s):
        rows_up = pl.ds(pl.multiple_of(chunk * 96, 48), 48)
        rows_dn = pl.ds(pl.multiple_of(chunk * 96 + 48, 48), 48)
        return (
            pltpu.make_async_copy(gathered.at[:, rows_up, :], up_s.at[s], wsem.at[s, 0]),
            pltpu.make_async_copy(gathered.at[:, rows_dn, :], dn_s.at[s], wsem.at[s, 1]),
        )

    def grad_copies(chunk, s):
        rows = pl.ds(pl.multiple_of(chunk * 96, 96), 96)
        return (
            pltpu.make_async_copy(gbuf.at[s, :, core], g_mine.at[:, rows, :], gsem.at[s, 0]),
            pltpu.make_async_copy(gbuf.at[s, :, 1 - core], g_theirs.at[:, rows, :], gsem.at[s, 1]),
        )

    @pl.when(c == 0)
    def _():
        for copy in weight_copies(0, 0):
            copy.start()
        proj_copy = pltpu.make_async_copy(gathered.at[:, pl.ds(384, 48), :], proj_s, psem)
        proj_copy.start()
        for src, where in ((tok_own, idx[16]), (tok_rx, 1 - idx[16])):
            base = pl.multiple_of(where * half, half)
            mid_s[pl.ds(base, half), :] = src[...].astype(F32)
        for src, where in ((cot_own, idx[16]), (cot_rx, 1 - idx[16])):
            base = pl.multiple_of(where * half, half)
            cot_s[pl.ds(base, half), :] = src[...]
        for j, a in enumerate((att0, att1, att2)):
            att_s[:, 256 * j : 256 * j + 256] = a[...]
        proj_copy.wait()
        proj = proj_s[...].reshape(768, 768)
        for i in range(0, seq, block):
            rows = slice(i, i + block)
            mid = mid_s[rows, :] + (dot(att_s[rows, :], proj) + small[6:7])
            mid_s[rows, :] = mid
            nhat, _rstd = norm_stats(mid)
            nm_s[rows, :] = (nhat * small[1:2] + small[3:4]).astype(BF16)
        nmt_s[...] = nm_s[...].T
        oacc[...] = jnp.zeros_like(oacc)
        dacc[...] = jnp.zeros_like(dacc)

    for copy in weight_copies(c, slot):
        copy.wait()

    @pl.when(c + 1 < n_c)
    def _():
        for copy in weight_copies(c + 1, 1 - slot):
            copy.start()

    up = up_s[slot].reshape(768, 768)
    dn = dn_s[slot].reshape(768, 768)
    bias = small[pl.ds(8 + c, 1), :]
    bias_sum = None
    for i in range(0, seq, block):
        rows = slice(i, i + block)
        pre = dot(nm_s[rows, :], up) + bias
        cdf = 0.5 * (1.0 + lax.erf(pre * 0.7071067811865476))
        act = (pre * cdf).astype(BF16)
        act_s[rows, :] = act
        oacc[rows, :] += dot(act, dn)
        slope = cdf + pre * (jnp.exp(pre * pre * -0.5) * 0.3989422804014327)
        d_pre = (dot(cot_s[rows, :], dn, NT) * slope).astype(BF16)
        dp_s[rows, :] = d_pre
        part = row_sum(d_pre.astype(F32))
        bias_sum = part if bias_sum is None else bias_sum + part
        dacc[rows, :] += dot(d_pre, up, NT)
    sums_o[pl.ds(8 + c, 1), :] = bias_sum

    @pl.when(c >= 2)
    def _():
        for copy in grad_copies(c - 2, slot):
            copy.wait()

    g_up = dot(nmt_s[...], dp_s[...]).astype(BF16).reshape(BLOCKS // 2, 2, 48, 768)
    gbuf[slot, :, :, 0:48, :] = g_up
    g_dn = dot(act_s[...], cot_s[...], TN).astype(BF16).reshape(BLOCKS // 2, 2, 48, 768)
    gbuf[slot, :, :, 48:96, :] = g_dn
    for copy in grad_copies(c, slot):
        copy.start()

    @pl.when(c == n_c - 1)
    def _():
        proj = proj_s[...].reshape(768, 768)
        gain_sum = shift_sum = bout_sum = bdown_sum = None
        for i in range(0, seq, block):
            rows = slice(i, i + block)
            mid = mid_s[rows, :]
            cot = cot_s[rows, :].astype(F32)
            d_nm = dacc[rows, :]
            nhat, rstd = norm_stats(mid)
            d_mid = cot + norm_back(d_nm * small[1:2], nhat, rstd)
            dmid_o[rows, :] = d_mid
            d_branch = d_mid.astype(BF16)
            dbr_s[rows, :] = d_branch
            datt_o[rows, :] = dot(d_branch, proj, NT).astype(BF16)
            parts = [row_sum(d_nm * nhat), row_sum(d_nm), row_sum(d_branch.astype(F32)), row_sum(cot)]
            if gain_sum is None:
                gain_sum, shift_sum, bout_sum, bdown_sum = parts
            else:
                gain_sum, shift_sum = gain_sum + parts[0], shift_sum + parts[1]
                bout_sum, bdown_sum = bout_sum + parts[2], bdown_sum + parts[3]
        sums_o[0:8, :] = jnp.concatenate(
            [jnp.zeros_like(gain_sum), gain_sum, jnp.zeros_like(gain_sum), shift_sum,
             jnp.zeros_like(gain_sum), jnp.zeros_like(gain_sum), bout_sum, bdown_sum], axis=0)
        sums_o[12:16, :] = jnp.zeros((4, 768), F32)
        for dst, where in ((lo_mine, idx[16]), (lo_theirs, 1 - idx[16])):
            base = pl.multiple_of(where * half, half)
            for i in range(0, half, block):
                rows = pl.ds(base + i, block)
                dst[i : i + block, :] = (mid_s[rows, :] + (oacc[rows, :] + small[7:8])).astype(BF16)
        gproj[...] = dot(att_s[...], dbr_s[...], TN).astype(BF16).reshape(BLOCKS // 2, 2, 48, 768)
        last = [
            pltpu.make_async_copy(gproj.at[:, core], g_mine.at[:, pl.ds(384, 48), :], gpsem.at[0]),
            pltpu.make_async_copy(gproj.at[:, 1 - core], g_theirs.at[:, pl.ds(384, 48), :], gpsem.at[1]),
        ]
        for copy in last:
            copy.start()
        for copy in grad_copies(c - 1, 1 - slot):
            copy.wait()
        for copy in grad_copies(c, slot):
            copy.wait()
        for copy in last:
            copy.wait()


def ffn(idx, gathered, atts, tok_own, tok_rx, cot_own, cot_rx, small):
    seq = 2 * tok_own.shape[0]
    sds = jax.ShapeDtypeStruct
    v = pltpu.VMEM
    half = tok_own.shape
    rows, frows = v((seq, 768), BF16), v((seq, 768), F32)
    return pl.pallas_call(
        functools.partial(ffn_body, 256),
        grid=(4,),
        in_specs=[SMEM, ANY] + [full((seq, 256))] * 3 + [full(half)] * 4 + [full((16, 768))],
        out_specs=[full(half), full(half), full((seq, 768)), full((seq, 768)), ANY, ANY, full((16, 768))],
        out_shape=[
            sds(half, BF16), sds(half, BF16), sds((seq, 768), F32), sds((seq, 768), BF16),
            sds((BLOCKS // 2, 432, 768), BF16), sds((BLOCKS // 2, 432, 768), BF16), sds((16, 768), F32),
        ],
        scratch_shapes=[
            v((2, BLOCKS, 48, 768), BF16), v((2, BLOCKS, 48, 768), BF16), v((BLOCKS, 48, 768), BF16),
            rows, frows, rows, v((768, seq), BF16), rows, rows, rows, frows, frows, rows,
            v((2, BLOCKS // 2, 2, 96, 768), BF16), v((BLOCKS // 2, 2, 48, 768), BF16),
            pltpu.SemaphoreType.DMA((2, 2)), pltpu.SemaphoreType.DMA, pltpu.SemaphoreType.DMA((2, 2)),
            pltpu.SemaphoreType.DMA((2,)),
        ],
        compiler_params=params(),
        cost_estimate=cost(50),
    )(idx, gathered, *atts, tok_own, tok_rx, cot_own, cot_rx, small)


def attn_backward_body(quad, last, block, idx, *refs):
    (q_i, k_i, v_i, o_i, do_i, li_i, e_i, w_i, nrm_i) = refs[:9]
    refs = refs[9:]
    if quad > 0:
        dni_i, refs = refs[0], refs[1:]
    if quad == 1:
        refs = refs[2:]
    if last:
        (tok_own, tok_rx, dmid_i, small, sums_i, b0, b1, gt_mine, gt_theirs, g_mine, g_theirs) = refs[:11]
        refs = refs[11:]
    else:
        (dni_o, b_o, g_mine, g_theirs) = refs[:4]
        refs = refs[4:]
    (vv, kk, dd, qm, dm, dkt, dvt, dj, nt, gbuf, sem) = refs[:11]
    pair = pl.program_id(0)
    seq = q_i.shape[0]
    half = seq // 2
    core = idx[17]
    zero = jnp.zeros((seq, 128), BF16)
    lane = lax.broadcasted_iota(jnp.int32, (seq, 128), 1)

    @pl.when(pair == 0)
    def _():
        nt[...] = nrm_i[...].T

    d_out = do_i[...].astype(F32) * li_i[...]
    d_low = d_out.astype(BF16)
    prod = d_out * o_i[...].astype(F32)
    extra = jnp.zeros((seq, 128), F32)
    for h in range(2):
        mine = (lane // HD) == h
        delta = jnp.sum(jnp.where(mine, prod, 0.0), axis=1, keepdims=True)
        high = delta.astype(BF16).astype(F32)
        extra = jnp.where(lane == 2 * h, -high, extra)
        extra = jnp.where(lane == 2 * h + 1, high - delta, extra)
        vv[h, :, 0:128] = jnp.where(mine, v_i[...], zero)
        vv[h, :, 128:256] = jnp.where((lane // 2) == h, 1.0, 0.0).astype(BF16)
        kk[h] = jnp.where(mine, k_i[...], zero)
        qm[h] = jnp.where(mine, q_i[...], zero).astype(F32).T.astype(BF16)
        dm[h] = jnp.where(mine, d_low, zero).astype(F32).T.astype(BF16)
    dd[:, 0:128] = d_low
    dd[:, 128:256] = extra.astype(BF16)
    base = pl.multiple_of(pair * 128, 128)
    for i in range(0, seq, block):
        rows = slice(i, i + block)
        dq = None
        for h in range(2):
            dp = dot(dd[rows, :], vv[h], NT)
            e = e_i[h, rows, :]
            ds = dp.astype(BF16) * e
            t = dot(ds, kk[h])
            dq = t if dq is None else dq + t
            a, b = dot(qm[h, :, rows], ds), dot(dm[h, :, rows], e)
            if i == 0 and h == 0:
                dkt[...], dvt[...] = a, b
            else:
                dkt[...] += a
                dvt[...] += b
        dj[rows, pl.ds(base, 128)] = (dq * 0.125).astype(BF16)
    dj[:, pl.ds(base + 256, 128)] = (dkt[...] * 0.125).T.astype(BF16)
    dj[:, pl.ds(base + 512, 128)] = dvt[...].T.astype(BF16)

    @pl.when(pair == 1)
    def _():
        g_rows = 48 if last else 48
        gbuf[:, :, 0:48, :] = dot(nt[...], dj[...]).astype(BF16).reshape(BLOCKS // 2, 2, 48, 768)
        bq, bv = row_sum(dj[:, 0:256].astype(F32)), row_sum(dj[:, 512:768].astype(F32))
        dst_rows = pl.ds(48 * quad, g_rows) if not last else pl.ds(0, 48)
        copies = [
            pltpu.make_async_copy(gbuf.at[:, core], g_mine.at[:, dst_rows, :], sem.at[0]),
            pltpu.make_async_copy(gbuf.at[:, 1 - core], g_theirs.at[:, dst_rows, :], sem.at[1]),
        ]
        for copy in copies:
            copy.start()
        weight = w_i[...]
        if not last:
            b_o[...] = jnp.concatenate([bq, bv, jnp.zeros((6, 256), F32)], axis=0)
            for i in range(0, seq, block):
                rows = slice(i, i + block)
                d_ni = dot(dj[rows, :], weight, NT)
                dni_o[rows, :] = d_ni if quad == 0 else dni_i[rows, :] + d_ni
        else:
            sbuf = refs[11]
            gain = small[0:1]
            gain_sum = shift_sum = None
            for src, dst, where in ((tok_rx, gt_theirs, 1 - idx[16]), (tok_own, gt_mine, idx[16])):
                start = pl.multiple_of(where * half, half)
                for i in range(0, half, block):
                    rows = pl.ds(start + i, block)
                    d_ni = dni_i[rows, :] + dot(dj[rows, :], weight, NT)
                    nhat, rstd = norm_stats(src[i : i + block, :].astype(F32))
                    grad = dmid_i[rows, :] + norm_back(d_ni * gain, nhat, rstd)
                    dst[i : i + block, :] = grad.astype(BF16)
                    parts = [row_sum(d_ni * nhat), row_sum(d_ni)]
                    if gain_sum is None:
                        gain_sum, shift_sum = parts
                    else:
                        gain_sum, shift_sum = gain_sum + parts[0], shift_sum + parts[1]
            sums = sums_i[...]
            row = lax.broadcasted_iota(jnp.int32, (16, 768), 0)
            sums = jnp.where(row == 0, gain_sum, sums)
            sums = jnp.where(row == 2, shift_sum, sums)
            sums = jnp.where(row == 4, jnp.concatenate([b0[0:1, :], b1[0:1, :], bq], axis=1), sums)
            sums = jnp.where(row == 5, jnp.concatenate([b0[1:2, :], b1[1:2, :], bv], axis=1), sums)
            low = sums.astype(BF16)
            for t in range(BLOCKS // 2):
                sbuf[t] = low
            more = [
                pltpu.make_async_copy(sbuf, g_mine.at[:, pl.ds(48, 16), :], sem.at[2]),
                pltpu.make_async_copy(sbuf, g_theirs.at[:, pl.ds(48, 16), :], sem.at[3]),
            ]
            for copy in more:
                copy.start()
            for copy in more:
                copy.wait()
        for copy in copies:
            copy.wait()


def attn_backward(quad, idx, heads, d_att, nrm, d_ni=None, grads=None, tail=None):
    last = tail is not None
    q, k, v, att, li, e, w = heads
    seq = q.shape[0]
    half = (seq // 2, 768)
    sds = jax.ShapeDtypeStruct
    vm = pltpu.VMEM
    pair_block = pl.BlockSpec((seq, 128), lambda p: (0, p))
    args = [idx, q, k, v, att, d_att, li, e, w, nrm]
    in_specs = [SMEM] + [pair_block] * 4 + [pl.BlockSpec((seq, 128), lambda p: (0, 2 * quad + p)), pair_block]
    in_specs += [pl.BlockSpec((2, seq, seq), lambda p: (p, 0, 0)), full(w.shape), full(nrm.shape)]
    alias = {}
    if quad > 0:
        args.append(d_ni)
        in_specs.append(full(d_ni.shape))
        if not last:
            alias[len(args) - 1] = 0
    if quad == 1:
        for j, g in enumerate(grads):
            args.append(g)
            in_specs.append(ANY)
            alias[len(args) - 1] = 2 + j
    if last:
        args += list(tail)
        in_specs += [full(a.shape) for a in tail]
        g_rows = 64
        out_shape = [sds(half, BF16), sds(half, BF16)]
        out_specs = [full(half), full(half)]
    else:
        g_rows = 96
        out_shape = [sds((seq, 768), F32), sds((8, 256), F32)]
        out_specs = [full((seq, 768)), full((8, 256))]
    out_shape += [sds((BLOCKS // 2, g_rows, 768), BF16)] * 2
    out_specs += [ANY, ANY]
    scratch = [
        vm((2, seq, 256), BF16), vm((2, seq, 128), BF16), vm((seq, 256), BF16), vm((2, 128, seq), BF16),
        vm((2, 128, seq), BF16), vm((128, seq), F32), vm((128, seq), F32), vm((seq, 768), BF16),
        vm((768, seq), BF16), vm((BLOCKS // 2, 2, 48, 768), BF16), pltpu.SemaphoreType.DMA((4,)),
    ]
    if last:
        scratch.append(vm((BLOCKS // 2, 16, 768), BF16))
    return pl.pallas_call(
        functools.partial(attn_backward_body, quad, last, 256),
        grid=(2,),
        in_specs=in_specs,
        out_specs=out_specs,
        out_shape=out_shape,
        scratch_shapes=scratch,
        input_output_aliases=alias,
        compiler_params=params(),
        cost_estimate=cost(15),
    )(*args)


def chip_cycle(n_chips):
    rows = n_chips // 2
    return [2 * i for i in range(rows)] + [2 * i + 1 for i in reversed(range(rows))]


def chip_shift(n_chips, step):
    order = chip_cycle(n_chips)
    return [
        (2 * order[i] + core, 2 * order[(i + step) % n_chips] + core)
        for i in range(n_chips)
        for core in (0, 1)
    ]


def core_swap(n_dev):
    return [(i, i ^ 1) for i in range(n_dev)]


def ring_gather(x, n_chips):
    ahead, behind = [x], [x]
    for t in range(n_chips // 2):
        ahead.append(lax.ppermute(ahead[-1], "dp", chip_shift(n_chips, 1)))
        if t < n_chips - 1 - n_chips // 2:
            behind.append(lax.ppermute(behind[-1], "dp", chip_shift(n_chips, -1)))
    own = jnp.stack(ahead + behind[1:])
    return own, lax.ppermute(own, "dp", core_swap(2 * n_chips))


def ring_order(n_chips):
    order = chip_cycle(n_chips)
    table = np.zeros((2 * n_chips, 2 * n_chips), np.int32)
    steps = list(range(0, -(n_chips // 2) - 1, -1)) + list(range(1, n_chips - n_chips // 2))
    for chip in range(n_chips):
        pos = order.index(chip)
        chips = [order[(pos + s) % n_chips] for s in steps]
        for core in (0, 1):
            table[2 * chip + core] = [2 * q + core for q in chips] + [2 * q + 1 - core for q in chips]
    return table


def ring_reduce(mine, theirs, n_chips):
    order = np.array(chip_cycle(n_chips), np.int32)
    position = np.argsort(order).astype(np.int32)
    pos = jnp.asarray(position)[lax.axis_index("dp") // 2]
    sib = lax.ppermute(theirs, "dp", core_swap(2 * n_chips))

    def term(step):
        chip = jnp.asarray(order)[lax.rem(pos + step + n_chips, n_chips)]
        a = lax.dynamic_index_in_dim(mine, chip, 0, keepdims=False)
        b = lax.dynamic_index_in_dim(sib, chip, 0, keepdims=False)
        return a.astype(F32) + b.astype(F32)

    ahead_steps, behind_steps = n_chips // 2, n_chips - 1 - n_chips // 2
    ahead = term(ahead_steps).astype(BF16)
    behind = term(-behind_steps).astype(BF16)
    for t in range(ahead_steps - 1, -1, -1):
        ahead = lax.ppermute(ahead, "dp", chip_shift(n_chips, 1))
        if t > 0:
            ahead = (ahead.astype(F32) + term(t)).astype(BF16)
        if t < behind_steps:
            behind = lax.ppermute(behind, "dp", chip_shift(n_chips, -1))
            if t > 0:
                behind = (behind.astype(F32) + term(-t)).astype(BF16)
    return (term(0) + ahead.astype(F32) + behind.astype(F32)).astype(BF16)


def swap_rows(x):
    return lax.ppermute(x, "blk", [(0, 1), (1, 0)])


def pack_weights(qkv_w, proj_w, up_w, down_w, shares):
    r = qkv_w.shape[0] // shares
    qkv = qkv_w.reshape(shares, r, 3, 3, 256).transpose(0, 3, 1, 2, 4).reshape(shares, 3, r, 768)
    up = up_w.reshape(shares, r, BLOCKS, 4, 48).transpose(0, 3, 1, 2, 4).reshape(shares, 4, 1, r, 768)
    down = down_w.reshape(shares, 4, 1, r, 768)
    up_down = jnp.concatenate([up, down], axis=2).reshape(shares, 8, r, 768)
    proj = proj_w.reshape(shares, 1, r, 768)
    return qkv, jnp.concatenate([up_down, proj], axis=1)


def pack_small(gains, shifts, qv_b, out_b, up_b, at):
    width = gains.shape[1]
    flat = jnp.concatenate([gains, shifts, qv_b, out_b, up_b.reshape(4, width)], axis=0)
    return lax.dynamic_update_slice(jnp.zeros((16, 768), flat.dtype), flat, (0, at))


def unpack_qkv(blocks, rows):
    return blocks.reshape(3, rows, 3, 256).transpose(1, 2, 0, 3).reshape(rows, 2304)


def unpack_up(blocks, rows):
    return blocks.reshape(4, rows, BLOCKS, 48).transpose(1, 2, 0, 3).reshape(rows, 3072)


def shards(tokens, segment_ids, padding_mask, qkv_weight, proj_weight, up_weight, down_weight,
           norm_gain, norm_shift, qv_bias, out_bias, up_bias, cotangent):
    n_dev = lax.axis_size("dp")
    dp, blk = lax.axis_index("dp"), lax.axis_index("blk")
    ring = n_dev == BLOCKS
    n_chips = BLOCKS // 2

    def pick(pair, which):
        return lax.dynamic_index_in_dim(pair, which, 0, keepdims=False)

    tok_own, tok_rx = pick(tokens, blk)[0], swap_rows(pick(tokens, 1 - blk)[0])
    cot_own = pick(cotangent, blk)[0]
    seg, pad = pick(segment_ids, blk)[0], pick(padding_mask, blk)[0]
    lanes = jnp.arange(128, dtype=jnp.int32)[None, :]
    code = jnp.where(lanes < 32, seg[:, None] // 32 == lanes, seg[:, None] % 32 + 32 == lanes)
    seg_q = code.astype(BF16)
    allowed = code & (pad[:, None] == 1)
    seg_k = jnp.where(allowed | (lanes >= 64), 0.0, MASKED).astype(BF16)

    if ring:
        qkv_blocks, rest = pack_weights(qkv_weight, proj_weight, up_weight, down_weight, 1)
        small = pack_small(norm_gain, norm_shift, qv_bias, out_bias, up_bias, 48 * dp)
        first = jnp.concatenate([qkv_blocks.reshape(144, 768), small], axis=0)
        own, sib = ring_gather(first, n_chips)
        gathered = lax.all_gather(rest.reshape(432, 768), "dp", axis=0)
        order = jnp.asarray(ring_order(n_chips))[dp]
        core = lax.rem(dp, 2)
    else:
        whole = [lax.all_gather(w, "dp", axis=0, tiled=True)
                 for w in (qkv_weight, proj_weight, up_weight, down_weight)]
        qkv_blocks, rest = pack_weights(*whole, BLOCKS)
        vectors = [lax.all_gather(w, "dp", axis=1, tiled=True)
                   for w in (norm_gain, norm_shift, qv_bias, out_bias)]
        hidden = lax.all_gather(up_bias, "dp", axis=0, tiled=True)
        hidden = hidden.reshape(BLOCKS, 4, 48).transpose(1, 0, 2).reshape(-1)
        small = pack_small(*vectors, hidden, 0)
        small = jnp.concatenate([small[None], jnp.zeros((BLOCKS - 1, 16, 768), BF16)], axis=0)
        first = jnp.concatenate([qkv_blocks.reshape(BLOCKS, 144, 768), small], axis=1)
        own, sib = first[:n_chips], first[n_chips:]
        gathered = rest.reshape(BLOCKS, 432, 768)
        order = jnp.arange(BLOCKS, dtype=jnp.int32)
        core = jnp.int32(0)
    idx = jnp.concatenate([order, jnp.stack([blk, core]).astype(jnp.int32)])
    cot_rx = swap_rows(pick(cotangent, 1 - blk)[0])

    outs = attn_forward(0, idx, own, sib, (tok_own, tok_rx), seg_q, seg_k)
    heads, nrm, small_all = [outs[:7]], outs[7], outs[8]
    for quad in (1, 2):
        heads.append(attn_forward(quad, idx, own, sib, (nrm, small_all), seg_q, seg_k))
    lo_mine, lo_theirs, d_mid, d_att, g_mine, g_theirs, sums = ffn(
        idx, gathered, [h[3] for h in heads], tok_own, tok_rx, cot_own, cot_rx, small_all)
    lo_rx = swap_rows(lo_theirs)

    d_ni, b0, q_mine, q_theirs = attn_backward(0, idx, heads[0], d_att, nrm)
    d_ni, b1, q_mine, q_theirs = attn_backward(1, idx, heads[1], d_att, nrm, d_ni, (q_mine, q_theirs))
    gt_mine, gt_theirs, l_mine, l_theirs = attn_backward(
        2, idx, heads[2], d_att, nrm, d_ni, tail=(tok_own, tok_rx, d_mid, small_all, sums, b0, b1))
    gt_rx = swap_rows(gt_theirs)

    def together(own_half, other_half):
        swapped = blk == 1
        return jnp.stack([jnp.where(swapped, other_half, own_half),
                          jnp.where(swapped, own_half, other_half)])[:, None]

    layer_out, grad_tokens = together(lo_mine, lo_rx), together(gt_mine, gt_rx)

    if ring:
        done = [ring_reduce(a, b, n_chips) for a, b in ((g_mine, g_theirs), (q_mine, q_theirs), (l_mine, l_theirs))]
        done = [d.astype(F32) + swap_rows(d).astype(F32) for d in done]
        r = 48
        ffn_blocks = done[0][0:384].reshape(4, 2, r, 768)
        g_up, g_down, g_proj = ffn_blocks[:, 0], ffn_blocks[:, 1].reshape(4 * r, 768), done[0][384:432]
        g_qkv = jnp.stack([done[1][0:48], done[1][48:96], done[2][0:48]])
        g_small = lax.dynamic_slice_in_dim(done[2][48:64], 48 * dp, 48, 1)
        width = 48
        return (layer_out, grad_tokens, unpack_qkv(g_qkv, r), g_proj, unpack_up(g_up, r), g_down,
                g_small[0:2], g_small[2:4], g_small[4:6], g_small[6:8], g_small[8:12].reshape(4 * width))

    def whole_sum(a, b):
        return jnp.stack([a, b], axis=1).reshape(BLOCKS, a.shape[1], 768)

    def scatter(x, dim):
        part = lax.psum_scatter(x, "dp", scatter_dimension=dim, tiled=True)
        return lax.psum(part.astype(BF16), "blk").astype(F32)

    g_ffn, g_q, g_l = whole_sum(g_mine, g_theirs), whole_sum(q_mine, q_theirs), whole_sum(l_mine, l_theirs)
    ffn_blocks = g_ffn[:, 0:384].reshape(BLOCKS, 4, 2, 48, 768).transpose(1, 2, 0, 3, 4).reshape(4, 2, 768, 768)
    g_up = unpack_up(ffn_blocks[:, 0], 768)
    g_down = ffn_blocks[:, 1].reshape(4, BLOCKS, 48, 768).transpose(1, 0, 2, 3).reshape(3072, 768)
    g_proj = g_ffn[:, 384:432].reshape(768, 768)
    g_qkv = jnp.stack([g_q[:, 0:48].reshape(768, 768), g_q[:, 48:96].reshape(768, 768),
                       g_l[:, 0:48].reshape(768, 768)])
    g_small = l_mine[0, 48:64].astype(F32)
    g_bias = g_small[8:12].reshape(4, BLOCKS, 48).transpose(1, 0, 2).reshape(-1)
    big = [scatter(g.astype(F32), 0) for g in (unpack_qkv(g_qkv, 768), g_proj, g_up, g_down)]
    return (layer_out, grad_tokens, *big,
            *[scatter(g_small[2 * i : 2 * i + 2], 1) for i in range(4)], scatter(g_bias, 0))


def solution(mesh):
    rows = P(None, "dp", "blk", None)
    return jax.shard_map(
        shards,
        mesh=mesh,
        in_specs=(rows, P(None, "dp", None), P(None, "dp", None)) + (P("dp", None),) * 4
        + (P(None, "dp"),) * 4 + (P("dp"), rows),
        out_specs=(rows, rows) + (P("dp", None),) * 4 + (P(None, "dp"),) * 4 + (P("dp"),),
        check_vma=False,
    )
```

time: 1370 us -> 393 us (0.29)
  waiting for transfers between devices: 593 us -> 97.6 us
  matrix products: 432 us -> 0 us
  blocking collectives: 176 us -> 0 us
  Pallas kernels: 0 us -> 152 us
  starting transfers between devices: 1.31 us -> 53.1 us
  local copies, waits for them, and re-layouts: 71.5 us -> 25.6 us
  other arithmetic: 62.3 us -> 24.2 us
  between operations: 17.2 us -> 35.8 us
    dot_general x192 -> x0, matrix products: 432 us -> none  [the longest x48 79.8 us: masked_scores(): jnp.einsum('rqd,rkd->rqk', query_one, key_one, preferred_element_type=jnp...]
    reduce_scatter x8 -> x0, waiting for transfers between devices: 355 us -> none  [the longest x1 114 us: reduce_owned(): lax.psum_scatter(terms[3], 'dp', scatter_dimension=0, tiled=True)]
    unnamed x25 -> x1, waiting for transfers between devices: 173 us -> 0.02 us
    pallas_call x0 -> x7, Pallas kernels: none -> 152 us  [the longest x3 59.9 us: attn_backward(): pl.pallas_call(functools.partial(attn_backward_body, quad, last, 256), gr...]
    ppermute x0 -> x39, waiting for transfers between devices: none -> 97.6 us  [the longest x12 40.5 us: ring_reduce(): ahead = lax.ppermute(ahead, 'dp', chip_shift(n_chips, 1))]
    unnamed x2 -> x0, blocking collectives: 93.9 us -> none
    all_gather x4 -> x0, blocking collectives: 76.9 us -> none  [the longest x1 23.1 us: fetch_weights(): lax.all_gather(norm_gain, 'dp', axis=1, tiled=True)]
    ppermute x0 -> x39, starting transfers between devices: none -> 53.1 us  [the longest x12 20.3 us: ring_reduce(): ahead = lax.ppermute(ahead, 'dp', chip_shift(n_chips, 1))]
  transfers between devices with their start and end apart: 21 -> 40, of which waited for: 13 -> 17; matrix products, arithmetic and copies ran while one was open for 29% -> 10% of each run, Pallas kernels for 0% -> 27%
where the time goes in v1:
time: 393 us; the launch traced here: 388 us
  Pallas kernels  152 us (39%)
  waiting for transfers between devices  97.6 us (25%)
  starting transfers between devices  53.1 us (14%)
  between operations  35.8 us (9%)
  local copies, waits for them, and re-layouts  25.6 us (7%)
  other arithmetic  24.2 us (6%)
    pallas_call x3, Pallas kernels, attn_backward(): pl.pallas_call(functools.partial(attn_backward_body, quad, last, 256), gr...  59.9 us
    pallas_call x1, Pallas kernels, ffn(): pl.pallas_call(functools.partial(ffn_body, 256), grid=(4,), in_specs=[SME...  48.3 us
    pallas_call x3, Pallas kernels, attn_forward(): pl.pallas_call(functools.partial(attn_forward_body, quad, 256), grid=(2,)...  43.8 us
    ppermute x12, waiting for transfers between devices, ring_reduce(): ahead = lax.ppermute(ahead, 'dp', chip_shift(n_chips, 1))  40.5 us
    ppermute x7, waiting for transfers between devices, swap_rows(): return lax.ppermute(x, 'blk', [(0, 1), (1, 0)])  27 us
    ppermute x4, waiting for transfers between devices, ring_gather(): ahead.append(lax.ppermute(ahead[-1], 'dp', chip_shift(n_chips, 1)))  26.5 us
    ppermute x12, starting transfers between devices, ring_reduce(): ahead = lax.ppermute(ahead, 'dp', chip_shift(n_chips, 1))  20.3 us
    ppermute x4, starting transfers between devices, ring_gather(): ahead.append(lax.ppermute(ahead[-1], 'dp', chip_shift(n_chips, 1)))  16.8 us
  transfers between devices with their start and end apart: 40, of which 17 were waited for; matrix products, arithmetic and copies ran while one was open for 10% of the time, Pallas kernels for 27%

profile of v1, /device:TPU:0, one launch (start us, length us, event | category | flops | bytes accessed | tf_op | source)
XLA Modules:
  0.0 388.3 jit_solution(2750682894114553247)
XLA Ops:
  12.8 3.4 collective-permute-start
  16.2 5.9 %collective-permute-done = bf16[160,768]{1,0:T(8,128)(2,1)S(1)} collective-permute-done((bf16[160,768]{1,0:T(8,128)(2,1)S(1)}, bf16[160,768]{1,0:T(8,128)(2,1)S(1)}, u32[]{:S(2)}, u32[]{:S(2)}) %collective-permute-start) | collective-permute-done | bytes 245792 | tf_op jit(solution)/shard_map/ppermute | solution.py:547
  24.1 10.5 %collective-permute-done.1 = bf16[160,768]{1,0:T(8,128)(2,1)S(1)} collective-permute-done((bf16[160,768]{1,0:T(8,128)(2,1)S(1)}, bf16[160,768]{1,0:T(8,128)(2,1)S(1)}, u32[]{:S(2)}, u32[]{:S(2)}) %collective-permute-start.1) | collective-permute-done | bytes 245792 | tf_op jit(solution)/shard_map/ppermute | solution.py:547
  34.6 6.1 %collective-permute-start.2 = (bf16[160,768]{1,0:T(8,128)(2,1)S(1)}, bf16[160,768]{1,0:T(8,128)(2,1)S(1)}, u32[]{:S(2)}, u32[]{:S(2)}) collective-permute-start(bf16[160,768]{1,0:T(8,128)(2,1)S(1)} %collective-permute-done.1), channel_id=1, source_target_pairs={{0,8},{2,10},{8,16},{10,18},{16,24},{18,26},{24,28},{26,30},{28,20... | collective-permute-start | bytes 737288 | tf_op jit(solution)/shard_map/ppermute | solution.py:547
  43.8 7.4 %collective-permute-done.2 = bf16[160,768]{1,0:T(8,128)(2,1)S(1)} collective-permute-done((bf16[160,768]{1,0:T(8,128)(2,1)S(1)}, bf16[160,768]{1,0:T(8,128)(2,1)S(1)}, u32[]{:S(2)}, u32[]{:S(2)}) %collective-permute-start.2) | collective-permute-done | bytes 245792 | tf_op jit(solution)/shard_map/ppermute | solution.py:547
  51.2 5.5 %collective-permute-start.3 = (bf16[160,768]{1,0:T(8,128)(2,1)S(1)}, bf16[160,768]{1,0:T(8,128)(2,1)S(1)}, u32[]{:S(2)}, u32[]{:S(2)}) collective-permute-start(bf16[160,768]{1,0:T(8,128)(2,1)S(1)} %collective-permute-done.2), channel_id=1, source_target_pairs={{0,8},{2,10},{8,16},{10,18},{16,24},{18,26},{24,28},{26,30},{28,20... | collective-permute-start | bytes 737288 | tf_op jit(solution)/shard_map/ppermute | solution.py:547
  60.3 2.7 collective-permute-done.3
  74.3 13.1 %collective-permute-done.8.refs_3_.tok_rx.refs_11_ = bf16[512,768]{1,0:T(8,128)(2,1)S(1)} collective-permute-done((bf16[512,768]{1,0:T(8,128)(2,1)S(1)}, bf16[512,768]{1,0:T(8,128)(2,1)S(1)}, u32[]{:S(2)}, u32[]{:S(2)}) %collective-permute-start.8) | collective-permute-done | bytes 786464 | tf_op jit(solution)/shard_map/ppermute | solution.py:593
  88.3 15.3 %shard_map.275 = (bf16[1024,256]{1,0:T(8,128)(2,1)}, bf16[1024,256]{1,0:T(8,128)(2,1)}, bf16[1024,256]{1,0:T(8,128)(2,1)}, bf16[1024,256]{1,0:T(8,128)(2,1)}, f3...) custom-call(s32[18]{0:T(128)} %pad_add_fusion.idx, ...), custom_call_target="tpu_custom_call" | custom-call | flops 12099999744 | bytes 1048576 | tf_op jit(solution)/shard_map/pallas_call | solution.py:174
  103.6 14.1 %shard_map.277 = (bf16[1024,256]{1,0:T(8,128)(2,1)}, bf16[1024,256]{1,0:T(8,128)(2,1)}, bf16[1024,256]{1,0:T(8,128)(2,1)}, bf16[1024,256]{1,0:T(8,128)(2,1)}, f3...) custom-call(s32[18]{0:T(128)} %pad_add_fusion.idx, ...), custom_call_target="tpu_custom_call" | custom-call | flops 12099999744 | bytes 1048576 | tf_op jit(solution)/shard_map/pallas_call | solution.py:174
  117.7 14.4 %shard_map.276 = (bf16[1024,256]{1,0:T(8,128)(2,1)}, bf16[1024,256]{1,0:T(8,128)(2,1)}, bf16[1024,256]{1,0:T(8,128)(2,1)}, bf16[1024,256]{1,0:T(8,128)(2,1)}, f3...) custom-call(s32[18]{0:T(128)} %pad_add_fusion.idx, ...), custom_call_target="tpu_custom_call" | custom-call | flops 12099999744 | bytes 1048576 | tf_op jit(solution)/shard_map/pallas_call | solution.py:174
  132.2 48.3 %shard_map.278 = (bf16[512,768]{1,0:T(8,128)(2,1)}, bf16[512,768]{1,0:T(8,128)(2,1)}, f32[1024,768]{1,0:T(8,128)}, bf16[1024,768]{1,0:T(8,128)(2,1)}, bf16[8,432...) custom-call(s32[18]{0:T(128)} %pad_add_fusion.idx, ...), custom_call_target="tpu_custom_call" | custom-call | flops 54999998464 | bytes 1048576 | tf_op jit(solution)/shard_map/pallas_call | solution.py:332
  180.6 18.2 %shard_map.279 = (f32[1024,768]{1,0:T(8,128)}, f32[8,256]{1,0:T(8,128)}, bf16[8,96,768]{2,1,0:T(8,128)(2,1)}, bf16[8,96,768]{2,1,0:T(8,128)(2,1)}) custom-call(s32[18]{0:T(128)} %pad_add_fusion.idx, bf16[1024,256]{1,0:T(8,128)(2,1)} %get-tuple-element.73.refs_0_, bf16[1024,256]{1,0:T(8,128)(2,1)} %get-tuple-element.74.refs_1_, ...), custom_call_target="tpu_custom_call" | custom-call | flops 16499999744 | bytes 1048576 | tf_op jit(solution)/shard_map/pallas_call | solution.py:513
  198.8 19.2 %shard_map.280 = (f32[1024,768]{1,0:T(8,128)}, f32[8,256]{1,0:T(8,128)}, bf16[8,96,768]{2,1,0:T(8,128)(2,1)}, bf16[8,96,768]{2,1,0:T(8,128)(2,1)}) custom-call(s32[18]{0:T(128)} %pad_add_fusion.idx, bf16[1024,256]{1,0:T(8,128)(2,1)} %get-tuple-element.67.refs_0_, ...), custom_call_target="tpu_custom_call", output_to_operand_aliasing={{0}: (10, {}), {2}: (11, {}), {3}: (12, {})} | custom-call | flops 16499999744 | bytes 1048576 | tf_op jit(solution)/shard_map/pallas_call | solution.py:513
  218.0 22.6 %shard_map.281 = (bf16[512,768]{1,0:T(8,128)(2,1)}, bf16[512,768]{1,0:T(8,128)(2,1)}, bf16[8,64,768]{2,1,0:T(8,128)(2,1)}, bf16[8,64,768]{2,1,0:T(8,128)(2,1)}) custom-call(s32[18]{0:T(128)} %pad_add_fusion.idx, bf16[1024,256]{1,0:T(8,128)(2,1)} %get-tuple-element.60.refs_0_, bf16[1024,256]{1,0:T(8,128)(2,1)} %get-tuple-element.61.refs_1_, ...), custom_call_target="tpu_custom_call" | custom-call | flops 16499999744 | bytes 1048576 | tf_op jit(solution)/shard_map/pallas_call | solution.py:513
  269.8 2.2 fusion.7
  273.8 4.1 %collective-permute-done.10 = bf16[512,768]{1,0:T(8,128)(2,1)} collective-permute-done((bf16[512,768]{1,0:T(8,128)(2,1)}, bf16[512,768]{1,0:T(8,128)(2,1)}, u32[]{:S(2)}, u32[]{:S(2)}) %collective-permute-start.10) | collective-permute-done | bytes 786464 | tf_op jit(solution)/shard_map/ppermute | solution.py:593
  282.5 7.3 %collective-permute-done.31 = bf16[432,768]{1,0:T(8,128)(2,1)S(1)} collective-permute-done((bf16[432,768]{1,0:T(8,128)(2,1)S(1)}, bf16[432,768]{1,0:T(8,128)(2,1)S(1)}, u32[]{:S(2)}, u32[]{:S(2)}) %collective-permute-start.31) | collective-permute-done | bytes 663584 | tf_op jit(solution)/shard_map/ppermute | solution.py:582
  296.4 11.8 %collective-permute-done.24 = bf16[64,768]{1,0:T(8,128)(2,1)S(1)} collective-permute-done((bf16[64,768]{1,0:T(8,128)(2,1)S(1)}, bf16[64,768]{1,0:T(8,128)(2,1)S(1)}, u32[]{:S(2)}, u32[]{:S(2)}) %collective-permute-start.24) | collective-permute-done | bytes 98336 | tf_op jit(solution)/shard_map/ppermute | solution.py:582
  320.9 11.8 %collective-permute-done.14 = bf16[96,768]{1,0:T(8,128)(2,1)S(1)} collective-permute-done((bf16[96,768]{1,0:T(8,128)(2,1)S(1)}, bf16[96,768]{1,0:T(8,128)(2,1)S(1)}, u32[]{:S(2)}, u32[]{:S(2)}) %collective-permute-start.14) | collective-permute-done | bytes 147488 | tf_op jit(solution)/shard_map/ppermute | solution.py:582
  334.9 3.0 fusion.2
  346.4 8.9 %collective-permute-done.16 = bf16[96,768]{1,0:T(8,128)(2,1)S(1)} collective-permute-done((bf16[96,768]{1,0:T(8,128)(2,1)}, bf16[96,768]{1,0:T(8,128)(2,1)S(1)}, u32[]{:S(2)}, u32[]{:S(2)}) %collective-permute-start.16) | collective-permute-done | bytes 147488 | tf_op jit(solution)/shard_map/ppermute | solution.py:582
  366.2 8.5 %collective-permute-done.38 = bf16[432,768]{1,0:T(8,128)(2,1)S(1)} collective-permute-done((bf16[432,768]{1,0:T(8,128)(2,1)S(1)}, bf16[432,768]{1,0:T(8,128)(2,1)S(1)}, u32[]{:S(2)}, u32[]{:S(2)}) %collective-permute-start.38) | collective-permute-done | bytes 663584 | tf_op jit(solution)/shard_map/ppermute | solution.py:593
  378.4 2.6 reshape.311
  (183 shorter events, 85.8 us)
Async XLA Ops:
  7.2 125.0 %all-gather.2.cloned.1.call-start = ((), (), s32[]{:S(2)}) async-start(), calls=%async_computation | async-start | bytes 11280384 | tf_op jit(solution)/shard_map/all_gather | solution.py:644
  23.9 18.1 %collective-permute-start.4 = (bf16[160,768]{1,0:T(8,128)(2,1)S(1)}, bf16[160,768]{1,0:T(8,128)(2,1)S(1)}, u32[]{:S(2)}, u32[]{:S(2)}) collective-permute-start(bf16[160,768]{1,0:T(8,128)(2,1)S(1)} %pad_maximum_fusion.2), channel_id=1, source_target_pairs={{0,4},{2,6},{8,0},{10,2},{16,8},{18,10},{24,16},{26,18},{28,24},{3... | collective-permute-start | bytes 737288 | tf_op jit(solution)/shard_map/ppermute | solution.py:549
  34.6 16.6 %collective-permute-start.2 = (bf16[160,768]{1,0:T(8,128)(2,1)S(1)}, bf16[160,768]{1,0:T(8,128)(2,1)S(1)}, u32[]{:S(2)}, u32[]{:S(2)}) collective-permute-start(bf16[160,768]{1,0:T(8,128)(2,1)S(1)} %collective-permute-done.1), channel_id=1, source_target_pairs={{0,8},{2,10},{8,16},{10,18},{16,24},{18,26},{24,28},{26,30},{28,20... | collective-permute-start | bytes 737288 | tf_op jit(solution)/shard_map/ppermute | solution.py:547
  42.0 15.4 %collective-permute-start.5 = (bf16[160,768]{1,0:T(8,128)(2,1)S(1)}, bf16[160,768]{1,0:T(8,128)(2,1)S(1)}, u32[]{:S(2)}, u32[]{:S(2)}) collective-permute-start(bf16[160,768]{1,0:T(8,128)(2,1)S(1)} %collective-permute-done.4), channel_id=1, source_target_pairs={{0,4},{2,6},{8,0},{10,2},{16,8},{18,10},{24,16},{26,18},{28,24},{3... | collective-permute-start | bytes 737288 | tf_op jit(solution)/shard_map/ppermute | solution.py:549
  66.1 21.3 %collective-permute-start.7 = (bf16[8,160,768]{2,1,0:T(8,128)(2,1)}, bf16[8,160,768]{2,1,0:T(8,128)(2,1)}, u32[]{:S(2)}, u32[]{:S(2)}) collective-permute-start(bf16[8,160,768]{2,1,0:T(8,128)(2,1)} %bitcast_dynamic-update-slice_fusion.refs_0_), channel_id=1, source_target_pairs={{0,2},{2,0},{4,6},{6,4},{8,10},{10,8},{12,14},{14,12},{16,18},{18,... | collective-permute-start | bytes 5898248 | tf_op jit(solution)/shard_map/ppermute | solution.py:551
  67.1 20.3 %collective-permute-start.8 = (bf16[512,768]{1,0:T(8,128)(2,1)S(1)}, bf16[512,768]{1,0:T(8,128)(2,1)S(1)}, u32[]{:S(2)}, u32[]{:S(2)}) collective-permute-start(bf16[512,768]{1,0:T(8,128)(2,1)S(1)} %get-tuple-element.152), channel_id=1, source_target_pairs={{0,1},{1,0},{2,3},{3,2},{4,5},{5,4},{6,7},{7,6},{8,9},{9,8},{10,11... | collective-permute-start | bytes 2359304 | tf_op jit(solution)/shard_map/ppermute | solution.py:593
  69.5 62.7 %collective-permute-start.9 = (bf16[512,768]{1,0:T(8,128)(2,1)S(1)}, bf16[512,768]{1,0:T(8,128)(2,1)}, u32[]{:S(2)}, u32[]{:S(2)}) collective-permute-start(bf16[512,768]{1,0:T(8,128)(2,1)S(1)} %get-tuple-element.150), channel_id=1, source_target_pairs={{0,1},{1,0},{2,3},{3,2},{4,5},{5,4},{6,7},{7,6},{8,9},{9,8},{10,11... | collective-permute-start | bytes 2359304 | tf_op jit(solution)/shard_map/ppermute | solution.py:593
  180.5 89.2 %collective-permute-start.30 = (bf16[8,432,768]{2,1,0:T(8,128)(2,1)}, bf16[8,432,768]{2,1,0:T(8,128)(2,1)}, u32[]{:S(2)}, u32[]{:S(2)}) collective-permute-start(bf16[8,432,768]{2,1,0:T(8,128)(2,1)} %get-tuple-element.94), channel_id=1, source_target_pairs={{0,2},{2,0},{4,6},{6,4},{8,10},{10,8},{12,14},{14,12},{16,18},{18,... | collective-permute-start | bytes 15925256 | tf_op jit(solution)/shard_map/ppermute | solution.py:570
  240.6 24.7 %collective-permute-start.21 = (bf16[8,64,768]{2,1,0:T(8,128)(2,1)}, bf16[8,64,768]{2,1,0:T(8,128)(2,1)S(1)}, u32[]{:S(2)}, u32[]{:S(2)}) collective-permute-start(bf16[8,64,768]{2,1,0:T(8,128)(2,1)} %get-tuple-element.92), channel_id=1, source_target_pairs={{0,2},{2,0},{4,6},{6,4},{8,10},{10,8},{12,14},{14,12},{16,18},{18,... | collective-permute-start | bytes 2359304 | tf_op jit(solution)/shard_map/ppermute | solution.py:570
  241.1 27.0 %collective-permute-start.11 = (bf16[512,768]{1,0:T(8,128)(2,1)}, bf16[512,768]{1,0:T(8,128)(2,1)}, u32[]{:S(2)}, u32[]{:S(2)}) collective-permute-start(bf16[512,768]{1,0:T(8,128)(2,1)} %get-tuple-element.87), channel_id=1, source_target_pairs={{0,1},{1,0},{2,3},{3,2},{4,5},{5,4},{6,7},{7,6},{8,9},{9,8},{10,11... | collective-permute-start | bytes 2359304 | tf_op jit(solution)/shard_map/ppermute | solution.py:593
  242.5 35.3 %collective-permute-start.10 = (bf16[512,768]{1,0:T(8,128)(2,1)}, bf16[512,768]{1,0:T(8,128)(2,1)}, u32[]{:S(2)}, u32[]{:S(2)}) collective-permute-start(bf16[512,768]{1,0:T(8,128)(2,1)} %get-tuple-element.58), channel_id=1, source_target_pairs={{0,1},{1,0},{2,3},{3,2},{4,5},{5,4},{6,7},{7,6},{8,9},{9,8},{10,11... | collective-permute-start | bytes 2359304 | tf_op jit(solution)/shard_map/ppermute | solution.py:593
  265.2 45.2 %collective-permute-start.12 = (bf16[8,96,768]{2,1,0:T(8,128)(2,1)}, bf16[8,96,768]{2,1,0:T(8,128)(2,1)S(1)}, u32[]{:S(2)}, u32[]{:S(2)}) collective-permute-start(bf16[8,96,768]{2,1,0:T(8,128)(2,1)} %get-tuple-element.90), channel_id=1, source_target_pairs={{0,2},{2,0},{4,6},{6,4},{8,10},{10,8},{12,14},{14,12},{16,18},{18,... | collective-permute-start | bytes 3538952 | tf_op jit(solution)/shard_map/ppermute | solution.py:570
  266.3 14.1 %collective-permute-start.22 = (bf16[64,768]{1,0:T(8,128)(2,1)S(1)}, bf16[64,768]{1,0:T(8,128)(2,1)S(1)}, u32[]{:S(2)}, u32[]{:S(2)}) collective-permute-start(bf16[64,768]{1,0:T(8,128)(2,1)S(1)} %get-tuple-element.144), channel_id=1, source_target_pairs={{0,8},{2,10},{8,16},{10,18},{16,24},{18,26},{24,28},{26,30},{28,20... | collective-permute-start | bytes 294920 | tf_op jit(solution)/shard_map/ppermute | solution.py:582
  268.1 24.9 %collective-permute-start.26 = (bf16[64,768]{1,0:T(8,128)(2,1)S(1)}, bf16[64,768]{1,0:T(8,128)(2,1)S(1)}, u32[]{:S(2)}, u32[]{:S(2)}) collective-permute-start(bf16[64,768]{1,0:T(8,128)(2,1)S(1)} %get-tuple-element.145), channel_id=1, source_target_pairs={{0,4},{2,6},{8,0},{10,2},{16,8},{18,10},{24,16},{26,18},{28,24},{3... | collective-permute-start | bytes 294920 | tf_op jit(solution)/shard_map/ppermute | solution.py:586
  271.9 17.8 %collective-permute-start.31 = (bf16[432,768]{1,0:T(8,128)(2,1)S(1)}, bf16[432,768]{1,0:T(8,128)(2,1)S(1)}, u32[]{:S(2)}, u32[]{:S(2)}) collective-permute-start(bf16[432,768]{1,0:T(8,128)(2,1)S(1)} %get-tuple-element.132), channel_id=1, source_target_pairs={{0,8},{2,10},{8,16},{10,18},{16,24},{18,26},{24,28},{26,30},{28,20... | collective-permute-start | bytes 1990664 | tf_op jit(solution)/shard_map/ppermute | solution.py:582
  282.3 30.1 %collective-permute-start.35 = (bf16[432,768]{1,0:T(8,128)(2,1)S(1)}, bf16[432,768]{1,0:T(8,128)(2,1)S(1)}, u32[]{:S(2)}, u32[]{:S(2)}) collective-permute-start(bf16[432,768]{1,0:T(8,128)(2,1)S(1)} %get-tuple-element.133), channel_id=1, source_target_pairs={{0,4},{2,6},{8,0},{10,2},{16,8},{18,10},{24,16},{26,18},{28,24},{3... | collective-permute-start | bytes 1990664 | tf_op jit(solution)/shard_map/ppermute | solution.py:586
  291.1 21.7 %collective-permute-start.32 = (bf16[432,768]{1,0:T(8,128)(2,1)S(1)}, bf16[432,768]{1,0:T(8,128)(2,1)S(1)}, u32[]{:S(2)}, u32[]{:S(2)}) collective-permute-start(bf16[432,768]{1,0:T(8,128)(2,1)S(1)} %fusion.4), channel_id=1, source_target_pairs={{0,8},{2,10},{8,16},{10,18},{16,24},{18,26},{24,28},{26,30},{28,20... | collective-permute-start | bytes 1990664 | tf_op jit(solution)/shard_map/ppermute | solution.py:582
  293.1 15.1 %collective-permute-start.24 = (bf16[64,768]{1,0:T(8,128)(2,1)S(1)}, bf16[64,768]{1,0:T(8,128)(2,1)S(1)}, u32[]{:S(2)}, u32[]{:S(2)}) collective-permute-start(bf16[64,768]{1,0:T(8,128)(2,1)S(1)} %get-tuple-element.142), channel_id=1, source_target_pairs={{0,8},{2,10},{8,16},{10,18},{16,24},{18,26},{24,28},{26,30},{28,20... | collective-permute-start | bytes 294920 | tf_op jit(solution)/shard_map/ppermute | solution.py:582
  314.6 20.3 %collective-permute-start.33 = (bf16[432,768]{1,0:T(8,128)(2,1)S(1)}, bf16[432,768]{1,0:T(8,128)(2,1)S(1)}, u32[]{:S(2)}, u32[]{:S(2)}) collective-permute-start(bf16[432,768]{1,0:T(8,128)(2,1)S(1)} %get-tuple-element.130), channel_id=1, source_target_pairs={{0,8},{2,10},{8,16},{10,18},{16,24},{18,26},{24,28},{26,30},{28,20... | collective-permute-start | bytes 1990664 | tf_op jit(solution)/shard_map/ppermute | solution.py:582
  317.2 17.8 %collective-permute-start.36 = (bf16[432,768]{1,0:T(8,128)(2,1)S(1)}, bf16[432,768]{1,0:T(8,128)(2,1)S(1)}, u32[]{:S(2)}, u32[]{:S(2)}) collective-permute-start(bf16[432,768]{1,0:T(8,128)(2,1)S(1)} %get-tuple-element.131), channel_id=1, source_target_pairs={{0,4},{2,6},{8,0},{10,2},{16,8},{18,10},{24,16},{26,18},{28,24},{3... | collective-permute-start | bytes 1990664 | tf_op jit(solution)/shard_map/ppermute | solution.py:586
  319.4 24.9 %collective-permute-start.29 = (bf16[64,768]{1,0:T(8,128)(2,1)S(1)}, bf16[64,768]{1,0:T(8,128)(2,1)S(1)}, u32[]{:S(2)}, u32[]{:S(2)}) collective-permute-start(bf16[64,768]{1,0:T(8,128)(2,1)S(1)} %fusion.24), channel_id=1, source_target_pairs={{0,1},{1,0},{2,3},{3,2},{4,5},{5,4},{6,7},{7,6},{8,9},{9,8},{10,11... | collective-permute-start | bytes 294920 | tf_op jit(solution)/shard_map/ppermute | solution.py:593
  337.9 21.1 %collective-permute-start.34 = (bf16[432,768]{1,0:T(8,128)(2,1)}, bf16[432,768]{1,0:T(8,128)(2,1)S(1)}, u32[]{:S(2)}, u32[]{:S(2)}) collective-permute-start(bf16[432,768]{1,0:T(8,128)(2,1)} %get-tuple-element.128), channel_id=1, source_target_pairs={{0,8},{2,10},{8,16},{10,18},{16,24},{18,26},{24,28},{26,30},{28,20... | collective-permute-start | bytes 1990664 | tf_op jit(solution)/shard_map/ppermute | solution.py:582
  339.7 19.3 %collective-permute-start.37 = (bf16[432,768]{1,0:T(8,128)(2,1)}, bf16[432,768]{1,0:T(8,128)(2,1)}, u32[]{:S(2)}, u32[]{:S(2)}) collective-permute-start(bf16[432,768]{1,0:T(8,128)(2,1)} %get-tuple-element.129), channel_id=1, source_target_pairs={{0,4},{2,6},{8,0},{10,2},{16,8},{18,10},{24,16},{26,18},{28,24},{3... | collective-permute-start | bytes 1990664 | tf_op jit(solution)/shard_map/ppermute | solution.py:586
  360.9 13.9 %collective-permute-start.38 = (bf16[432,768]{1,0:T(8,128)(2,1)S(1)}, bf16[432,768]{1,0:T(8,128)(2,1)S(1)}, u32[]{:S(2)}, u32[]{:S(2)}) collective-permute-start(bf16[432,768]{1,0:T(8,128)(2,1)S(1)} %fusion.6), channel_id=1, source_target_pairs={{0,1},{1,0},{2,3},{3,2},{4,5},{5,4},{6,7},{7,6},{8,9},{9,8},{10,11... | collective-permute-start | bytes 1990664 | tf_op jit(solution)/shard_map/ppermute | solution.py:593
  (38 other events, 403.5 us)
Sparse Core Ops, SparseCore 0:
  11.8 103.5 all-gather.1

commit v2 on v1

--- a/solution.py
+++ b/solution.py
@@ -53,38 +53,45 @@
     return jnp.sum(x, axis=0, keepdims=True)
 
 
+def send_copies(idx, buf, rows, mine, near, far, sem):
+    core = idx[17]
+    copies = []
+    for slot in range(BLOCKS // 2):
+        chip = idx[18 + slot]
+        theirs = near.at[slot] if slot < 2 else far.at[slot - 2]
+        copies.append(pltpu.make_async_copy(buf.at[chip, core], mine.at[slot, rows, :], sem.at[0, slot]))
+        copies.append(pltpu.make_async_copy(buf.at[chip, 1 - core], theirs.at[rows, :], sem.at[1, slot]))
+    return copies
+
+
+def send_shapes(rows):
+    return [jax.ShapeDtypeStruct((n, rows, 768), BF16) for n in (BLOCKS // 2, 2, BLOCKS // 2 - 2)]
+
+
 def attn_forward_body(quad, block, idx, *refs):
     first = quad == 0
+    parts, refs = refs[:BLOCKS], refs[BLOCKS:]
     if first:
-        (own, sib, tok_own, tok_rx, sq, sk, q_o, k_o, v_o, att_o, li_o, e_o, w_o, nrm_o, small_o,
+        (tok_own, tok_rx, sq, sk, q_o, k_o, v_o, att_o, li_o, e_o, w_o, nrm_o, small_o,
          w_s, s_s, kk, vv, aa, sem) = refs
     else:
-        (own, sib, nrm_i, small_i, sq, sk, q_o, k_o, v_o, att_o, li_o, e_o, w_o,
+        (nrm_i, small_i, sq, sk, q_o, k_o, v_o, att_o, li_o, e_o, w_o,
          w_s, kk, vv, aa, sem) = refs
     seq = sq.shape[0]
     half = seq // 2
-    n_part = own.shape[0]
     pair = pl.program_id(0)
 
     @pl.when(pair == 0)
     def _():
         copies = []
-        for j, part in enumerate((own, sib)):
-            for t in range(n_part):
-                at = idx[j * n_part + t]
+        for t, part in enumerate(parts):
+            copies.append(
+                pltpu.make_async_copy(part.at[pl.ds(48 * quad, 48), :], w_s.at[idx[t]], sem.at[0, t])
+            )
+            if first:
                 copies.append(
-                    pltpu.make_async_copy(
-                        part.at[t, pl.ds(48 * quad, 48), :], w_s.at[at], sem.at[0, j * n_part + t]
-                    )
+                    pltpu.make_async_copy(part.at[pl.ds(144, 16), :], s_s.at[t], sem.at[1, t])
                 )
-                if first:
-                    copies.append(
-                        pltpu.make_async_copy(
-                            part.at[t, pl.ds(144, 16), :],
-                            s_s.at[j * n_part + t],
-                            sem.at[1, j * n_part + t],
-                        )
-                    )
         for c in copies:
             c.start()
         for c in copies:
@@ -93,7 +100,7 @@
         w_o[...] = weight
         if first:
             small = jnp.zeros((16, 768), F32)
-            for t in range(2 * n_part):
+            for t in range(BLOCKS):
                 small = small + s_s[t].astype(F32)
             small_o[...] = small
             gain, shift = small[0:1], small[2:3]
@@ -141,7 +148,7 @@
         att_o[rows, :] = (acc[:, 0:128] * inverse).astype(BF16)
 
 
-def attn_forward(quad, idx, own, sib, rows_in, sq, sk):
+def attn_forward(quad, idx, parts, rows_in, sq, sk):
     seq = sq.shape[0]
     sds = jax.ShapeDtypeStruct
     first = quad == 0
@@ -174,7 +181,7 @@
     return pl.pallas_call(
         functools.partial(attn_forward_body, quad, 256),
         grid=(2,),
-        in_specs=[SMEM, ANY, ANY]
+        in_specs=[SMEM] + [ANY] * BLOCKS
         + [full(r.shape) for r in rows_in]
         + [full(sq.shape), full(sk.shape)],
         out_specs=out_specs,
@@ -182,12 +189,19 @@
         scratch_shapes=scratch,
         compiler_params=params(),
         cost_estimate=cost(11),
-    )(idx, own, sib, *rows_in, sq, sk)
+    )(idx, *parts, *rows_in, sq, sk)
 
 
 def ffn_body(
-    block, idx, gathered, att0, att1, att2, tok_own, tok_rx, cot_own, cot_rx, small,
-    lo_mine, lo_theirs, dmid_o, datt_o, g_mine, g_theirs, sums_o,
+    block, idx, *refs
+):
+    parts, refs = refs[:BLOCKS], refs[BLOCKS:]
+    ffn_steps(block, idx, parts, *refs)
+
+
+def ffn_steps(
+    block, idx, parts, att0, att1, att2, tok_own, tok_rx, cot_own, cot_rx, small,
+    lo_mine, lo_theirs, dmid_o, datt_o, g_mine, g_near, g_far, sums_o,
     up_s, dn_s, proj_s, att_s, mid_s, nm_s, nmt_s, cot_s, act_s, dp_s, oacc, dacc, dbr_s, gbuf, gproj,
     wsem, psem, gsem, gpsem,
 ):
@@ -196,29 +210,30 @@
     slot = lax.rem(c, 2)
     seq = mid_s.shape[0]
     half = seq // 2
-    core = idx[17]
 
     def weight_copies(chunk, s):
         rows_up = pl.ds(pl.multiple_of(chunk * 96, 48), 48)
         rows_dn = pl.ds(pl.multiple_of(chunk * 96 + 48, 48), 48)
-        return (
-            pltpu.make_async_copy(gathered.at[:, rows_up, :], up_s.at[s], wsem.at[s, 0]),
-            pltpu.make_async_copy(gathered.at[:, rows_dn, :], dn_s.at[s], wsem.at[s, 1]),
-        )
+        return [
+            pltpu.make_async_copy(part.at[rows, :], buf.at[s, idx[t]], wsem.at[s, j, t])
+            for t, part in enumerate(parts)
+            for j, (rows, buf) in enumerate(((rows_up, up_s), (rows_dn, dn_s)))
+        ]
 
     def grad_copies(chunk, s):
         rows = pl.ds(pl.multiple_of(chunk * 96, 96), 96)
-        return (
-            pltpu.make_async_copy(gbuf.at[s, :, core], g_mine.at[:, rows, :], gsem.at[s, 0]),
-            pltpu.make_async_copy(gbuf.at[s, :, 1 - core], g_theirs.at[:, rows, :], gsem.at[s, 1]),
-        )
+        return send_copies(idx, gbuf.at[s], rows, g_mine, g_near, g_far, gsem.at[s])
 
     @pl.when(c == 0)
     def _():
         for copy in weight_copies(0, 0):
             copy.start()
-        proj_copy = pltpu.make_async_copy(gathered.at[:, pl.ds(384, 48), :], proj_s, psem)
-        proj_copy.start()
+        proj_copies = [
+            pltpu.make_async_copy(part.at[pl.ds(384, 48), :], proj_s.at[idx[t]], psem.at[t])
+            for t, part in enumerate(parts)
+        ]
+        for copy in proj_copies:
+            copy.start()
         for src, where in ((tok_own, idx[16]), (tok_rx, 1 - idx[16])):
             base = pl.multiple_of(where * half, half)
             mid_s[pl.ds(base, half), :] = src[...].astype(F32)
@@ -227,7 +242,8 @@
             cot_s[pl.ds(base, half), :] = src[...]
         for j, a in enumerate((att0, att1, att2)):
             att_s[:, 256 * j : 256 * j + 256] = a[...]
-        proj_copy.wait()
+        for copy in proj_copies:
+            copy.wait()
         proj = proj_s[...].reshape(768, 768)
         for i in range(0, seq, block):
             rows = slice(i, i + block)
@@ -309,10 +325,7 @@
                 rows = pl.ds(base + i, block)
                 dst[i : i + block, :] = (mid_s[rows, :] + (oacc[rows, :] + small[7:8])).astype(BF16)
         gproj[...] = dot(att_s[...], dbr_s[...], TN).astype(BF16).reshape(BLOCKS // 2, 2, 48, 768)
-        last = [
-            pltpu.make_async_copy(gproj.at[:, core], g_mine.at[:, pl.ds(384, 48), :], gpsem.at[0]),
-            pltpu.make_async_copy(gproj.at[:, 1 - core], g_theirs.at[:, pl.ds(384, 48), :], gpsem.at[1]),
-        ]
+        last = send_copies(idx, gproj, pl.ds(384, 48), g_mine, g_near, g_far, gpsem)
         for copy in last:
             copy.start()
         for copy in grad_copies(c - 1, 1 - slot):
@@ -323,7 +336,7 @@
             copy.wait()
 
 
-def ffn(idx, gathered, atts, tok_own, tok_rx, cot_own, cot_rx, small):
+def ffn(idx, parts, atts, tok_own, tok_rx, cot_own, cot_rx, small):
     seq = 2 * tok_own.shape[0]
     sds = jax.ShapeDtypeStruct
     v = pltpu.VMEM
@@ -332,22 +345,22 @@
     return pl.pallas_call(
         functools.partial(ffn_body, 256),
         grid=(4,),
-        in_specs=[SMEM, ANY] + [full((seq, 256))] * 3 + [full(half)] * 4 + [full((16, 768))],
-        out_specs=[full(half), full(half), full((seq, 768)), full((seq, 768)), ANY, ANY, full((16, 768))],
+        in_specs=[SMEM] + [ANY] * BLOCKS + [full((seq, 256))] * 3 + [full(half)] * 4 + [full((16, 768))],
+        out_specs=[full(half), full(half), full((seq, 768)), full((seq, 768)), ANY, ANY, ANY, full((16, 768))],
         out_shape=[
             sds(half, BF16), sds(half, BF16), sds((seq, 768), F32), sds((seq, 768), BF16),
-            sds((BLOCKS // 2, 432, 768), BF16), sds((BLOCKS // 2, 432, 768), BF16), sds((16, 768), F32),
+            *send_shapes(432), sds((16, 768), F32),
         ],
         scratch_shapes=[
             v((2, BLOCKS, 48, 768), BF16), v((2, BLOCKS, 48, 768), BF16), v((BLOCKS, 48, 768), BF16),
             rows, frows, rows, v((768, seq), BF16), rows, rows, rows, frows, frows, rows,
             v((2, BLOCKS // 2, 2, 96, 768), BF16), v((BLOCKS // 2, 2, 48, 768), BF16),
-            pltpu.SemaphoreType.DMA((2, 2)), pltpu.SemaphoreType.DMA, pltpu.SemaphoreType.DMA((2, 2)),
-            pltpu.SemaphoreType.DMA((2,)),
+            pltpu.SemaphoreType.DMA((2, 2, BLOCKS)), pltpu.SemaphoreType.DMA((BLOCKS,)),
+            pltpu.SemaphoreType.DMA((2, 2, BLOCKS // 2)), pltpu.SemaphoreType.DMA((2, BLOCKS // 2)),
         ],
         compiler_params=params(),
         cost_estimate=cost(50),
-    )(idx, gathered, *atts, tok_own, tok_rx, cot_own, cot_rx, small)
+    )(idx, *parts, *atts, tok_own, tok_rx, cot_own, cot_rx, small)
 
 
 def attn_backward_body(quad, last, block, idx, *refs):
@@ -355,19 +368,17 @@
     refs = refs[9:]
     if quad > 0:
         dni_i, refs = refs[0], refs[1:]
-    if quad == 1:
-        refs = refs[2:]
+        refs = refs[3:]
     if last:
-        (tok_own, tok_rx, dmid_i, small, sums_i, b0, b1, gt_mine, gt_theirs, g_mine, g_theirs) = refs[:11]
-        refs = refs[11:]
+        (tok_own, tok_rx, dmid_i, small, sums_i, b0, b1, gt_mine, gt_theirs, *sends) = refs[:12]
+        refs = refs[12:]
     else:
-        (dni_o, b_o, g_mine, g_theirs) = refs[:4]
-        refs = refs[4:]
+        (dni_o, b_o, *sends) = refs[:5]
+        refs = refs[5:]
     (vv, kk, dd, qm, dm, dkt, dvt, dj, nt, gbuf, sem) = refs[:11]
     pair = pl.program_id(0)
     seq = q_i.shape[0]
     half = seq // 2
-    core = idx[17]
     zero = jnp.zeros((seq, 128), BF16)
     lane = lax.broadcasted_iota(jnp.int32, (seq, 128), 1)
 
@@ -414,14 +425,9 @@
 
     @pl.when(pair == 1)
     def _():
-        g_rows = 48 if last else 48
-        gbuf[:, :, 0:48, :] = dot(nt[...], dj[...]).astype(BF16).reshape(BLOCKS // 2, 2, 48, 768)
+        gbuf[...] = dot(nt[...], dj[...]).astype(BF16).reshape(BLOCKS // 2, 2, 48, 768)
         bq, bv = row_sum(dj[:, 0:256].astype(F32)), row_sum(dj[:, 512:768].astype(F32))
-        dst_rows = pl.ds(48 * quad, g_rows) if not last else pl.ds(0, 48)
-        copies = [
-            pltpu.make_async_copy(gbuf.at[:, core], g_mine.at[:, dst_rows, :], sem.at[0]),
-            pltpu.make_async_copy(gbuf.at[:, 1 - core], g_theirs.at[:, dst_rows, :], sem.at[1]),
-        ]
+        copies = send_copies(idx, gbuf, pl.ds(48 * quad, 48), *sends, sem.at[0])
         for copy in copies:
             copy.start()
         weight = w_i[...]
@@ -456,11 +462,8 @@
             sums = jnp.where(row == 5, jnp.concatenate([b0[1:2, :], b1[1:2, :], bv], axis=1), sums)
             low = sums.astype(BF16)
             for t in range(BLOCKS // 2):
-                sbuf[t] = low
-            more = [
-                pltpu.make_async_copy(sbuf, g_mine.at[:, pl.ds(48, 16), :], sem.at[2]),
-                pltpu.make_async_copy(sbuf, g_theirs.at[:, pl.ds(48, 16), :], sem.at[3]),
-            ]
+                sbuf[t, 0], sbuf[t, 1] = low, low
+            more = send_copies(idx, sbuf, pl.ds(144, 16), *sends, sem.at[1])
             for copy in more:
                 copy.start()
             for copy in more:
@@ -486,7 +489,6 @@
         in_specs.append(full(d_ni.shape))
         if not last:
             alias[len(args) - 1] = 0
-    if quad == 1:
         for j, g in enumerate(grads):
             args.append(g)
             in_specs.append(ANY)
@@ -494,22 +496,20 @@
     if last:
         args += list(tail)
         in_specs += [full(a.shape) for a in tail]
-        g_rows = 64
         out_shape = [sds(half, BF16), sds(half, BF16)]
         out_specs = [full(half), full(half)]
     else:
-        g_rows = 96
         out_shape = [sds((seq, 768), F32), sds((8, 256), F32)]
         out_specs = [full((seq, 768)), full((8, 256))]
-    out_shape += [sds((BLOCKS // 2, g_rows, 768), BF16)] * 2
-    out_specs += [ANY, ANY]
+    out_shape += send_shapes(160)
+    out_specs += [ANY, ANY, ANY]
     scratch = [
         vm((2, seq, 256), BF16), vm((2, seq, 128), BF16), vm((seq, 256), BF16), vm((2, 128, seq), BF16),
         vm((2, 128, seq), BF16), vm((128, seq), F32), vm((128, seq), F32), vm((seq, 768), BF16),
-        vm((768, seq), BF16), vm((BLOCKS // 2, 2, 48, 768), BF16), pltpu.SemaphoreType.DMA((4,)),
+        vm((768, seq), BF16), vm((BLOCKS // 2, 2, 48, 768), BF16), pltpu.SemaphoreType.DMA((2, 2, BLOCKS // 2)),
     ]
     if last:
-        scratch.append(vm((BLOCKS // 2, 16, 768), BF16))
+        scratch.append(vm((BLOCKS // 2, 2, 16, 768), BF16))
     return pl.pallas_call(
         functools.partial(attn_backward_body, quad, last, 256),
         grid=(2,),
@@ -541,14 +541,28 @@
     return [(i, i ^ 1) for i in range(n_dev)]
 
 
-def ring_gather(x, n_chips):
-    ahead, behind = [x], [x]
-    for t in range(n_chips // 2):
-        ahead.append(lax.ppermute(ahead[-1], "dp", chip_shift(n_chips, 1)))
-        if t < n_chips - 1 - n_chips // 2:
-            behind.append(lax.ppermute(behind[-1], "dp", chip_shift(n_chips, -1)))
-    own = jnp.stack(ahead + behind[1:])
-    return own, lax.ppermute(own, "dp", core_swap(2 * n_chips))
+def tie(*arrays):
+    return lax.optimization_barrier(arrays)
+
+
+class RingGather:
+    def __init__(self, x, n_chips):
+        self.n, self.ahead, self.behind = n_chips, [x], [x]
+
+    def step(self):
+        if len(self.ahead) <= self.n // 2:
+            self.ahead.append(lax.ppermute(self.ahead[-1], "dp", chip_shift(self.n, 1)))
+        if len(self.behind) <= self.n - 1 - self.n // 2:
+            self.behind.append(lax.ppermute(self.behind[-1], "dp", chip_shift(self.n, -1)))
+
+    def tie(self, *arrays):
+        out = tie(self.ahead[-1], self.behind[-1], *arrays)
+        self.ahead[-1], self.behind[-1] = out[:2]
+        return out[2:]
+
+    def parts(self):
+        own = self.ahead + self.behind[1:]
+        return own + [lax.ppermute(x, "dp", core_swap(2 * self.n)) for x in own]
 
 
 def ring_order(n_chips):
@@ -563,30 +577,54 @@
     return table
 
 
-def ring_reduce(mine, theirs, n_chips):
-    order = np.array(chip_cycle(n_chips), np.int32)
-    position = np.argsort(order).astype(np.int32)
-    pos = jnp.asarray(position)[lax.axis_index("dp") // 2]
-    sib = lax.ppermute(theirs, "dp", core_swap(2 * n_chips))
-
-    def term(step):
-        chip = jnp.asarray(order)[lax.rem(pos + step + n_chips, n_chips)]
-        a = lax.dynamic_index_in_dim(mine, chip, 0, keepdims=False)
-        b = lax.dynamic_index_in_dim(sib, chip, 0, keepdims=False)
-        return a.astype(F32) + b.astype(F32)
-
-    ahead_steps, behind_steps = n_chips // 2, n_chips - 1 - n_chips // 2
-    ahead = term(ahead_steps).astype(BF16)
-    behind = term(-behind_steps).astype(BF16)
-    for t in range(ahead_steps - 1, -1, -1):
-        ahead = lax.ppermute(ahead, "dp", chip_shift(n_chips, 1))
-        if t > 0:
-            ahead = (ahead.astype(F32) + term(t)).astype(BF16)
-        if t < behind_steps:
-            behind = lax.ppermute(behind, "dp", chip_shift(n_chips, -1))
-            if t > 0:
-                behind = (behind.astype(F32) + term(-t)).astype(BF16)
-    return (term(0) + ahead.astype(F32) + behind.astype(F32)).astype(BF16)
+def send_order(n_chips):
+    order = chip_cycle(n_chips)
+    steps = []
+    for t in range(n_chips // 2, 0, -1):
+        steps += [t, 1 - t] if t > 1 else [t]
+    steps.append(0)
+    table = np.zeros((n_chips, n_chips), np.int32)
+    for chip in range(n_chips):
+        table[chip] = [order[(order.index(chip) + s) % n_chips] for s in steps]
+    return table
+
+
+class RingReduce:
+    def __init__(self, mine, near, far, n_chips):
+        self.n, self.mine, self.slot = n_chips, mine, 0
+        self.near = lax.ppermute(near, "dp", core_swap(2 * n_chips))
+        self.far = lax.ppermute(far, "dp", core_swap(2 * n_chips))
+        self.ahead, self.behind = self.term(), self.term()
+        self.left = n_chips // 2
+
+    def term(self, *moved):
+        other = self.near[self.slot] if self.slot < 2 else self.far[self.slot - 2]
+        total = self.mine[self.slot].astype(F32) + other.astype(F32)
+        for m in moved:
+            total = total + m.astype(F32)
+        self.slot += 1
+        return total.astype(BF16)
+
+    def send(self):
+        self.ahead, self.behind = tie(self.ahead, self.behind)
+        self.ahead = lax.ppermute(self.ahead, "dp", chip_shift(self.n, 1))
+        if self.left > 1:
+            self.behind = lax.ppermute(self.behind, "dp", chip_shift(self.n, -1))
+        self.left -= 1
+
+    def add(self):
+        if self.left > 1:
+            self.ahead = self.term(self.ahead)
+            self.behind = self.term(self.behind)
+        elif self.left == 1:
+            self.ahead = self.term(self.ahead)
+        else:
+            self.ahead = self.term(self.ahead, self.behind)
+
+    def tie(self, *arrays):
+        out = tie(self.ahead, self.behind, *arrays)
+        self.ahead, self.behind = out[:2]
+        return out[2:]
 
 
 def swap_rows(x):
@@ -628,7 +666,7 @@
         return lax.dynamic_index_in_dim(pair, which, 0, keepdims=False)
 
     tok_own, tok_rx = pick(tokens, blk)[0], swap_rows(pick(tokens, 1 - blk)[0])
-    cot_own = pick(cotangent, blk)[0]
+    cot_own, cot_send = pick(cotangent, blk)[0], pick(cotangent, 1 - blk)[0]
     seg, pad = pick(segment_ids, blk)[0], pick(padding_mask, blk)[0]
     lanes = jnp.arange(128, dtype=jnp.int32)[None, :]
     code = jnp.where(lanes < 32, seg[:, None] // 32 == lanes, seg[:, None] % 32 + 32 == lanes)
@@ -639,11 +677,16 @@
     if ring:
         qkv_blocks, rest = pack_weights(qkv_weight, proj_weight, up_weight, down_weight, 1)
         small = pack_small(norm_gain, norm_shift, qv_bias, out_bias, up_bias, 48 * dp)
-        first = jnp.concatenate([qkv_blocks.reshape(144, 768), small], axis=0)
-        own, sib = ring_gather(first, n_chips)
-        gathered = lax.all_gather(rest.reshape(432, 768), "dp", axis=0)
+        first = RingGather(jnp.concatenate([qkv_blocks.reshape(144, 768), small], axis=0), n_chips)
+        rest = rest.reshape(432, 768)
+        for _ in range(4):
+            first.step()
+        (rest,) = first.tie(rest)
+        parts = first.parts()
+        second = RingGather(rest, n_chips)
         order = jnp.asarray(ring_order(n_chips))[dp]
         core = lax.rem(dp, 2)
+        chips = jnp.asarray(send_order(n_chips))[dp // 2]
     else:
         whole = [lax.all_gather(w, "dp", axis=0, tiled=True)
                  for w in (qkv_weight, proj_weight, up_weight, down_weight)]
@@ -654,65 +697,97 @@
         hidden = hidden.reshape(BLOCKS, 4, 48).transpose(1, 0, 2).reshape(-1)
         small = pack_small(*vectors, hidden, 0)
         small = jnp.concatenate([small[None], jnp.zeros((BLOCKS - 1, 16, 768), BF16)], axis=0)
-        first = jnp.concatenate([qkv_blocks.reshape(BLOCKS, 144, 768), small], axis=1)
-        own, sib = first[:n_chips], first[n_chips:]
-        gathered = rest.reshape(BLOCKS, 432, 768)
+        parts = list(jnp.concatenate([qkv_blocks.reshape(BLOCKS, 144, 768), small], axis=1))
+        rest_parts = list(rest.reshape(BLOCKS, 432, 768))
         order = jnp.arange(BLOCKS, dtype=jnp.int32)
         core = jnp.int32(0)
-    idx = jnp.concatenate([order, jnp.stack([blk, core]).astype(jnp.int32)])
-    cot_rx = swap_rows(pick(cotangent, 1 - blk)[0])
-
-    outs = attn_forward(0, idx, own, sib, (tok_own, tok_rx), seg_q, seg_k)
-    heads, nrm, small_all = [outs[:7]], outs[7], outs[8]
+        chips = jnp.arange(n_chips, dtype=jnp.int32)
+    idx = jnp.concatenate([order, jnp.stack([blk, core]).astype(jnp.int32), chips])
+    cot_send, tok_rx = tie(cot_send, tok_rx)
+    cot_rx = swap_rows(cot_send)
+
+    if ring:
+        second.step()
+    outs = attn_forward(0, idx, parts, (tok_own, tok_rx), seg_q, seg_k)
+    heads, nrm, small_all = [list(outs[:7])], outs[7], outs[8]
     for quad in (1, 2):
-        heads.append(attn_forward(quad, idx, own, sib, (nrm, small_all), seg_q, seg_k))
-    lo_mine, lo_theirs, d_mid, d_att, g_mine, g_theirs, sums = ffn(
-        idx, gathered, [h[3] for h in heads], tok_own, tok_rx, cot_own, cot_rx, small_all)
+        if ring:
+            nrm, small_all, cot_rx, heads[-1][3] = second.tie(nrm, small_all, cot_rx, heads[-1][3])
+            second.step()
+        heads.append(list(attn_forward(quad, idx, parts, (nrm, small_all), seg_q, seg_k)))
+    atts = [h[3] for h in heads]
+    if ring:
+        atts[2], small_all = second.tie(atts[2], small_all)
+        second.step()
+        rest_parts = second.parts()
+    lo_mine, lo_theirs, d_mid, d_att, *sends, sums = ffn(
+        idx, rest_parts, atts, tok_own, tok_rx, cot_own, cot_rx, small_all)
     lo_rx = swap_rows(lo_theirs)
 
-    d_ni, b0, q_mine, q_theirs = attn_backward(0, idx, heads[0], d_att, nrm)
-    d_ni, b1, q_mine, q_theirs = attn_backward(1, idx, heads[1], d_att, nrm, d_ni, (q_mine, q_theirs))
-    gt_mine, gt_theirs, l_mine, l_theirs = attn_backward(
-        2, idx, heads[2], d_att, nrm, d_ni, tail=(tok_own, tok_rx, d_mid, small_all, sums, b0, b1))
-    gt_rx = swap_rows(gt_theirs)
+    if ring:
+        ffn_sum = RingReduce(*sends, n_chips)
+        (d_att,) = ffn_sum.tie(d_att)
+        ffn_sum.send()
+    d_ni, b0, *q_sends = attn_backward(0, idx, heads[0], d_att, nrm)
+    if ring:
+        d_ni, ffn_sum.far, lo_rx = ffn_sum.tie(d_ni, ffn_sum.far, lo_rx)
+        ffn_sum.add()
+        (d_ni,) = ffn_sum.tie(d_ni)
+        ffn_sum.send()
+    d_ni, b1, *q_sends = attn_backward(1, idx, heads[1], d_att, nrm, d_ni, q_sends)
+    if ring:
+        (d_ni,) = ffn_sum.tie(d_ni)
+        ffn_sum.add()
+        (d_ni,) = ffn_sum.tie(d_ni)
+        ffn_sum.send()
+    gt_mine, gt_theirs, *q_sends = attn_backward(
+        2, idx, heads[2], d_att, nrm, d_ni, q_sends, tail=(tok_own, tok_rx, d_mid, small_all, sums, b0, b1))
 
     def together(own_half, other_half):
         swapped = blk == 1
         return jnp.stack([jnp.where(swapped, other_half, own_half),
                           jnp.where(swapped, own_half, other_half)])[:, None]
 
-    layer_out, grad_tokens = together(lo_mine, lo_rx), together(gt_mine, gt_rx)
-
     if ring:
-        done = [ring_reduce(a, b, n_chips) for a, b in ((g_mine, g_theirs), (q_mine, q_theirs), (l_mine, l_theirs))]
-        done = [d.astype(F32) + swap_rows(d).astype(F32) for d in done]
+        gt_theirs, *q_sends = ffn_sum.tie(gt_theirs, *q_sends)
+        ffn_sum.add()
+        ffn_sum.send()
+        qkv_sum = RingReduce(*q_sends, n_chips)
+        gt_rx = swap_rows(gt_theirs)
+        qkv_sum.send()
+        ffn_sum.add()
+        for _ in range(3):
+            qkv_sum.add()
+            qkv_sum.send()
+        qkv_sum.add()
+        done_ffn, done_qkv = [x.ahead.astype(F32) + swap_rows(x.ahead).astype(F32) for x in (ffn_sum, qkv_sum)]
         r = 48
-        ffn_blocks = done[0][0:384].reshape(4, 2, r, 768)
-        g_up, g_down, g_proj = ffn_blocks[:, 0], ffn_blocks[:, 1].reshape(4 * r, 768), done[0][384:432]
-        g_qkv = jnp.stack([done[1][0:48], done[1][48:96], done[2][0:48]])
-        g_small = lax.dynamic_slice_in_dim(done[2][48:64], 48 * dp, 48, 1)
-        width = 48
-        return (layer_out, grad_tokens, unpack_qkv(g_qkv, r), g_proj, unpack_up(g_up, r), g_down,
-                g_small[0:2], g_small[2:4], g_small[4:6], g_small[6:8], g_small[8:12].reshape(4 * width))
-
-    def whole_sum(a, b):
-        return jnp.stack([a, b], axis=1).reshape(BLOCKS, a.shape[1], 768)
+        ffn_blocks = done_ffn[0:384].reshape(4, 2, r, 768)
+        g_up, g_down, g_proj = ffn_blocks[:, 0], ffn_blocks[:, 1].reshape(4 * r, 768), done_ffn[384:432]
+        g_small = lax.dynamic_slice_in_dim(done_qkv[144:160], 48 * dp, 48, 1)
+        return (together(lo_mine, lo_rx), together(gt_mine, gt_rx),
+                unpack_qkv(done_qkv[0:144], r), g_proj, unpack_up(g_up, r), g_down,
+                g_small[0:2], g_small[2:4], g_small[4:6], g_small[6:8], g_small[8:12].reshape(-1))
+
+    gt_rx = swap_rows(gt_theirs)
+
+    def whole_sum(mine, near, far):
+        return jnp.stack([mine, jnp.concatenate([near, far])], axis=1).reshape(BLOCKS, mine.shape[1], 768)
 
     def scatter(x, dim):
         part = lax.psum_scatter(x, "dp", scatter_dimension=dim, tiled=True)
         return lax.psum(part.astype(BF16), "blk").astype(F32)
 
-    g_ffn, g_q, g_l = whole_sum(g_mine, g_theirs), whole_sum(q_mine, q_theirs), whole_sum(l_mine, l_theirs)
+    g_ffn, g_q = whole_sum(*sends), whole_sum(*q_sends)
     ffn_blocks = g_ffn[:, 0:384].reshape(BLOCKS, 4, 2, 48, 768).transpose(1, 2, 0, 3, 4).reshape(4, 2, 768, 768)
     g_up = unpack_up(ffn_blocks[:, 0], 768)
     g_down = ffn_blocks[:, 1].reshape(4, BLOCKS, 48, 768).transpose(1, 0, 2, 3).reshape(3072, 768)
     g_proj = g_ffn[:, 384:432].reshape(768, 768)
-    g_qkv = jnp.stack([g_q[:, 0:48].reshape(768, 768), g_q[:, 48:96].reshape(768, 768),
-                       g_l[:, 0:48].reshape(768, 768)])
-    g_small = l_mine[0, 48:64].astype(F32)
+    g_qkv = jnp.stack([g_q[:, 48 * j : 48 * j + 48].reshape(768, 768) for j in range(3)])
+    g_small = g_q[0, 144:160].astype(F32)
     g_bias = g_small[8:12].reshape(4, BLOCKS, 48).transpose(1, 0, 2).reshape(-1)
     big = [scatter(g.astype(F32), 0) for g in (unpack_qkv(g_qkv, 768), g_proj, g_up, g_down)]
-    return (layer_out, grad_tokens, *big,
+    return (together(lo_mine, lo_rx), together(gt_mine, gt_rx), *big,
             *[scatter(g_small[2 * i : 2 * i + 2], 1) for i in range(4)], scatter(g_bias, 0))
 
 

time: 393 us -> 329 us (0.84)
  between operations: 35.8 us -> 1.58 us
  waiting for transfers between devices: 97.6 us -> 70.5 us
  Pallas kernels: 152 us -> 165 us
  starting transfers between devices: 53.1 us -> 41.5 us
  local copies, waits for them, and re-layouts: 25.6 us -> 21.5 us
    ppermute x7 -> x6, waiting for transfers between devices: 27 us -> 1.9 us  [swap_rows(): return lax.ppermute(x, 'blk', [(0, 1), (1, 0)])]
    pallas_call x1, Pallas kernels: 48.3 us -> 60.8 us  [ffn(): pl.pallas_call(functools.partial(ffn_body, 256), grid=(4,), in_specs=[SME...]
    ppermute x32 -> x48, starting transfers between devices: 45.3 us -> 35.3 us  [the longest x8 15.5 us: step(): self.ahead.append(lax.ppermute(self.ahead[-1], 'dp', chip_shift(self.n, 1)))]
    convert_element_type x15 -> x10, other arithmetic: 13.5 us -> 16.7 us  [term(): return total.astype(BF16)]
    ppermute x32 -> x48, waiting for transfers between devices: 70.5 us -> 68.6 us  [the longest x8 27.6 us: step(): self.ahead.append(lax.ppermute(self.ahead[-1], 'dp', chip_shift(self.n, 1)))]
  transfers between devices with their start and end apart: 40 -> 54, of which waited for: 17 -> 20; matrix products, arithmetic and copies ran while one was open for 10% -> 8% of each run, Pallas kernels for 27% -> 32%
where the time goes in v2:
time: 329 us; the launch traced here: 325 us
  Pallas kernels  165 us (50%)
  waiting for transfers between devices  70.5 us (21%)
  starting transfers between devices  41.5 us (13%)
  other arithmetic  25.1 us (8%)
  local copies, waits for them, and re-layouts  21.5 us (7%)
    pallas_call x1, Pallas kernels, ffn(): pl.pallas_call(functools.partial(ffn_body, 256), grid=(4,), in_specs=[SME...  60.8 us
    pallas_call x3, Pallas kernels, attn_backward(): pl.pallas_call(functools.partial(attn_backward_body, quad, last, 256), gr...  60.5 us
    pallas_call x3, Pallas kernels, attn_forward(): pl.pallas_call(functools.partial(attn_forward_body, quad, 256), grid=(2,)...  43.4 us
    ppermute x8, waiting for transfers between devices, step(): self.ahead.append(lax.ppermute(self.ahead[-1], 'dp', chip_shift(self.n, 1)))  27.6 us
    ppermute x8, waiting for transfers between devices, send(): self.ahead = lax.ppermute(self.ahead, 'dp', chip_shift(self.n, 1))  22.2 us
    convert_element_type x10, other arithmetic, term(): return total.astype(BF16)  16.7 us
    ppermute x8, starting transfers between devices, step(): self.ahead.append(lax.ppermute(self.ahead[-1], 'dp', chip_shift(self.n, 1)))  15.5 us
    ppermute x8, starting transfers between devices, send(): self.ahead = lax.ppermute(self.ahead, 'dp', chip_shift(self.n, 1))  12.2 us
  transfers between devices with their start and end apart: 54, of which 20 were waited for; matrix products, arithmetic and copies ran while one was open for 8% of the time, Pallas kernels for 32%

profile of v2, /device:TPU:0, one launch (start us, length us, event | category | flops | bytes accessed | tf_op | source)
XLA Modules:
  0.0 324.9 jit_solution(15278312473535169569)
XLA Ops:
  3.3 3.4 %collective-permute-start = (bf16[160,768]{1,0:T(8,128)(2,1)S(1)}, bf16[160,768]{1,0:T(8,128)(2,1)}, u32[]{:S(2)}, u32[]{:S(2)}) collective-permute-start(bf16[160,768]{1,0:T(8,128)(2,1)S(1)} %pad_maximum_fusion.2.refs_0_), channel_id=1, source_target_pairs={{0,8},{2,10},{8,16},{10,18},{16,24},{18,26},{24,28},{26,30},{28,20... | collective-permute-start | bytes 737288 | tf_op jit(solution)/shard_map/ppermute | solution.py:554
  15.1 6.1 %collective-permute-done.1.refs_2_ = bf16[160,768]{1,0:T(8,128)(2,1)S(1)} collective-permute-done((bf16[160,768]{1,0:T(8,128)(2,1)}, bf16[160,768]{1,0:T(8,128)(2,1)S(1)}, u32[]{:S(2)}, u32[]{:S(2)}) %collective-permute-start.1) | collective-permute-done | bytes 245792 | tf_op jit(solution)/shard_map/ppermute | solution.py:554
  24.1 4.6 %collective-permute-done.2.refs_3_ = bf16[160,768]{1,0:T(8,128)(2,1)S(1)} collective-permute-done((bf16[160,768]{1,0:T(8,128)(2,1)S(1)}, bf16[160,768]{1,0:T(8,128)(2,1)S(1)}, u32[]{:S(2)}, u32[]{:S(2)}) %collective-permute-start.2) | collective-permute-done | bytes 245792 | tf_op jit(solution)/shard_map/ppermute | solution.py:554
  33.5 3.6 %collective-permute-done.3.refs_4_ = bf16[160,768]{1,0:T(8,128)(2,1)S(1)} collective-permute-done((bf16[160,768]{1,0:T(8,128)(2,1)S(1)}, bf16[160,768]{1,0:T(8,128)(2,1)S(1)}, u32[]{:S(2)}, u32[]{:S(2)}) %collective-permute-start.3) | collective-permute-done | bytes 245792 | tf_op jit(solution)/shard_map/ppermute | solution.py:554
  43.9 15.3 %shard_map.230 = (bf16[1024,256]{1,0:T(8,128)(2,1)}, bf16[1024,256]{1,0:T(8,128)(2,1)}, bf16[1024,256]{1,0:T(8,128)(2,1)}, bf16[1024,256]{1,0:T(8,128)(2,1)}, f3...) custom-call(s32[26]{0:T(128)} %pad_add_fusion.idx, ...), custom_call_target="tpu_custom_call" | custom-call | flops 12099999744 | bytes 1048576 | tf_op jit(solution)/shard_map/pallas_call | solution.py:181
  60.2 2.1 collective-permute-start.19
  62.9 14.0 %shard_map.231 = (bf16[1024,256]{1,0:T(8,128)(2,1)}, bf16[1024,256]{1,0:T(8,128)(2,1)}, bf16[1024,256]{1,0:T(8,128)(2,1)}, bf16[1024,256]{1,0:T(8,128)(2,1)}, f3...) custom-call(s32[26]{0:T(128)} %pad_add_fusion.idx, bf16[160,768]{1,0:T(8,128)(2,1)} %copy-done.13, ...), custom_call_target="tpu_custom_call" | custom-call | flops 12099999744 | bytes 1048576 | tf_op jit(solution)/shard_map/pallas_call | solution.py:181
  77.0 3.0 collective-permute-done.20.refs_6_
  82.0 14.0 %shard_map.232 = (bf16[1024,256]{1,0:T(8,128)(2,1)}, bf16[1024,256]{1,0:T(8,128)(2,1)}, bf16[1024,256]{1,0:T(8,128)(2,1)}, bf16[1024,256]{1,0:T(8,128)(2,1)}, f3...) custom-call(s32[26]{0:T(128)} %pad_add_fusion.idx, bf16[160,768]{1,0:T(8,128)(2,1)} %copy-done.13, ...), custom_call_target="tpu_custom_call" | custom-call | flops 12099999744 | bytes 1048576 | tf_op jit(solution)/shard_map/pallas_call | solution.py:181
  100.8 12.6 %collective-permute-done.23.refs_4_ = bf16[432,768]{1,0:T(8,128)(2,1)S(1)} collective-permute-done((bf16[432,768]{1,0:T(8,128)(2,1)S(1)}, bf16[432,768]{1,0:T(8,128)(2,1)S(1)}, u32[]{:S(2)}, u32[]{:S(2)}) %collective-permute-start.23) | collective-permute-done | bytes 663584 | tf_op jit(solution)/shard_map/ppermute | solution.py:554
  116.4 60.8 %shard_map.233 = (bf16[512,768]{1,0:T(8,128)(2,1)}, bf16[512,768]{1,0:T(8,128)(2,1)}, f32[1024,768]{1,0:T(8,128)}, bf16[1024,768]{1,0:T(8,128)(2,1)}, bf16[8,432...) custom-call(s32[26]{0:T(128)} %pad_add_fusion.idx, ...), custom_call_target="tpu_custom_call" | custom-call | flops 54999998464 | bytes 1048576 | tf_op jit(solution)/shard_map/pallas_call | solution.py:345
  179.0 7.3 %collective-permute-done.32 = bf16[2,432,768]{2,1,0:T(8,128)(2,1)S(1)} collective-permute-done((bf16[2,432,768]{2,1,0:T(8,128)(2,1)}, bf16[2,432,768]{2,1,0:T(8,128)(2,1)S(1)}, u32[]{:S(2)}, u32[]{:S(2)}) %collective-permute-start.32) | collective-permute-done | bytes 1327136 | tf_op jit(solution)/shard_map/ppermute | solution.py:595
  186.3 2.7 fusion.8
  191.0 18.4 %shard_map.234 = (f32[1024,768]{1,0:T(8,128)}, f32[8,256]{1,0:T(8,128)}, bf16[8,160,768]{2,1,0:T(8,128)(2,1)}, bf16[2,160,768]{2,1,0:T(8,128)(2,1)}, bf16[6,160,768]{2,1,0:T(8,128)(2,1)}) custom-call(s32[26]{0:T(128)} %pad_add_fusion.idx, bf16[1024,256]{1,0:T(8,128)(2,1)} %get-tuple-element.150.refs_0_, bf16[1024,256]{1,0:T(8,128)(2,1)} %get-tuple-element.151.refs_1_, ...), custom_call_target="tpu_custom_call" | custom-call | flops 16499999744 | bytes 1048576 | tf_op jit(solution)/shard_map/pallas_call | solution.py:513
  209.5 4.7 %fusion.4 = (bf16[432,768]{1,0:T(8,128)(2,1)}, bf16[432,768]{1,0:T(8,128)(2,1)}) fusion(bf16[432,768]{1,0:T(8,128)(2,1)} %collective-permute-done.34, bf16[6,432,768]{2,1,0:T(8,128)(2,1)S(1)} %collective-permute-done.35, bf16[8,432,768]{2,1,0:T(8,128)(2,1)} %get-tuple-element.143, bf16[432,768]{1,0:T(8,128)(2,1)} %collective-permute-done.33), kind=kLoop, calls=%fused_computation.11 | loop fusion | flops 3981312 | bytes 5308416 | tf_op jit(solution)/shard_map/convert_element_type | solution.py:606
  216.2 19.3 %shard_map.235 = (f32[1024,768]{1,0:T(8,128)}, f32[8,256]{1,0:T(8,128)}, bf16[8,160,768]{2,1,0:T(8,128)(2,1)}, bf16[2,160,768]{2,1,0:T(8,128)(2,1)}, bf16[6,160,768]{2,1,0:T(8,128)(2,1)}) custom-call(s32[26]{0:T(128)} %pad_add_fusion.idx, ...), custom_call_target="tpu_custom_call", output_to_operand_aliasing={{0}: (10, {}), {2}: (11, {}), {3}: (12, {}), {4}: (13, {})} | custom-call | flops 16499999744 | bytes 1048576 | tf_op jit(solution)/shard_map/pallas_call | solution.py:513
  235.6 3.3 %fusion.3 = (bf16[432,768]{1,0:T(8,128)(2,1)}, bf16[432,768]{1,0:T(8,128)(2,1)}) fusion(bf16[432,768]{1,0:T(8,128)(2,1)} %collective-permute-done.38, bf16[6,432,768]{2,1,0:T(8,128)(2,1)S(1)} %collective-permute-done.35, bf16[8,432,768]{2,1,0:T(8,128)(2,1)} %get-tuple-element.143, bf16[432,768]{1,0:T(8,128)(2,1)} %collective-permute-done.37), kind=kLoop, calls=%fused_computation.9 | loop fusion | flops 3981312 | bytes 5308416 | tf_op jit(solution)/shard_map/convert_element_type | solution.py:606
  240.9 22.8 %shard_map.236 = (bf16[512,768]{1,0:T(8,128)(2,1)}, bf16[512,768]{1,0:T(8,128)(2,1)}, bf16[8,160,768]{2,1,0:T(8,128)(2,1)}, bf16[2,160,768]{2,1,0:T(8,128)(2,1)}, bf16[6,160,768]{2,1,0:T(8,128)(2,1)}) custom-call(s32[26]{0:T(128)} %pad_add_fusion.idx, ...), custom_call_target="tpu_custom_call", output_to_operand_aliasing={{2}: (11, {}), {3}: (12, {}), {4}: (13, {})} | custom-call | flops 16499999744 | bytes 1048576 | tf_op jit(solution)/shard_map/pallas_call | solution.py:513
  275.6 13.5 %collective-permute-done.44 = bf16[160,768]{1,0:T(8,128)(2,1)S(1)} collective-permute-done((bf16[160,768]{1,0:T(8,128)(2,1)S(1)}, bf16[160,768]{1,0:T(8,128)(2,1)S(1)}, u32[]{:S(2)}, u32[]{:S(2)}) %collective-permute-start.44) | collective-permute-done | bytes 245792 | tf_op jit(solution)/shard_map/ppermute | solution.py:610
  294.2 2.0 collective-permute-done.46
  301.3 2.8 collective-permute-done.48
  304.2 2.8 collective-permute-done.49
  309.4 4.0 %collective-permute-done.50 = bf16[160,768]{1,0:T(8,128)(2,1)S(1)} collective-permute-done((bf16[160,768]{1,0:T(8,128)(2,1)S(1)}, bf16[160,768]{1,0:T(8,128)(2,1)S(1)}, u32[]{:S(2)}, u32[]{:S(2)}) %collective-permute-start.50) | collective-permute-done | bytes 245792 | tf_op jit(solution)/shard_map/ppermute | solution.py:610
  317.9 2.6 reshape.238
  (232 shorter events, 77.5 us)
Async XLA Ops:
  6.7 30.4 %collective-permute-start.9 = (bf16[160,768]{1,0:T(8,128)(2,1)S(1)}, bf16[160,768]{1,0:T(8,128)(2,1)}, u32[]{:S(2)}, u32[]{:S(2)}) collective-permute-start(bf16[160,768]{1,0:T(8,128)(2,1)S(1)} %pad_maximum_fusion.2.refs_0_), channel_id=1, source_target_pairs={{0,2},{2,0},{4,6},{6,4},{8,10},{10,8},{12,14},{14,12},{16,18},{18,... | collective-permute-start | bytes 737288 | tf_op jit(solution)/shard_map/ppermute | solution.py:565
  7.9 30.2 %collective-permute-start.17 = (bf16[512,768]{1,0:T(8,128)(2,1)}, bf16[512,768]{1,0:T(8,128)(2,1)}, u32[]{:S(2)}, u32[]{:S(2)}) collective-permute-start(bf16[512,768]{1,0:T(8,128)(2,1)} %get-tuple-element.263), channel_id=1, source_target_pairs={{0,1},{1,0},{2,3},{3,2},{4,5},{5,4},{6,7},{7,6},{8,9},{9,8},{10,11... | collective-permute-start | bytes 2359304 | tf_op jit(solution)/shard_map/ppermute | solution.py:631
  40.3 19.9 %collective-permute-start.18 = (bf16[512,768]{1,0:T(8,128)(2,1)S(1)}, bf16[512,768]{1,0:T(8,128)(2,1)S(1)}, u32[]{:S(2)}, u32[]{:S(2)}) collective-permute-start(bf16[512,768]{1,0:T(8,128)(2,1)S(1)} %get-tuple-element.123), channel_id=1, source_target_pairs={{0,1},{1,0},{2,3},{3,2},{4,5},{5,4},{6,7},{7,6},{8,9},{9,8},{10,11... | collective-permute-start | bytes 2359304 | tf_op jit(solution)/shard_map/ppermute | solution.py:631
  40.4 19.9 %collective-permute-start.7 = (bf16[432,768]{1,0:T(8,128)(2,1)S(1)}, bf16[432,768]{1,0:T(8,128)(2,1)S(1)}, u32[]{:S(2)}, u32[]{:S(2)}) collective-permute-start(bf16[432,768]{1,0:T(8,128)(2,1)S(1)} %bitcast.118), channel_id=1, source_target_pairs={{0,8},{2,10},{8,16},{10,18},{16,24},{18,26},{24,28},{26,30},{28,20... | collective-permute-start | bytes 1990664 | tf_op jit(solution)/shard_map/ppermute | solution.py:554
  42.2 18.0 %collective-permute-start.8 = (bf16[432,768]{1,0:T(8,128)(2,1)S(1)}, bf16[432,768]{1,0:T(8,128)(2,1)}, u32[]{:S(2)}, u32[]{:S(2)}) collective-permute-start(bf16[432,768]{1,0:T(8,128)(2,1)S(1)} %bitcast.119), channel_id=1, source_target_pairs={{0,4},{2,6},{8,0},{10,2},{16,8},{18,10},{24,16},{26,18},{28,24},{3... | collective-permute-start | bytes 1990664 | tf_op jit(solution)/shard_map/ppermute | solution.py:556
  42.5 57.2 %collective-permute-start.24 = (bf16[432,768]{1,0:T(8,128)(2,1)S(1)}, bf16[432,768]{1,0:T(8,128)(2,1)}, u32[]{:S(2)}, u32[]{:S(2)}) collective-permute-start(bf16[432,768]{1,0:T(8,128)(2,1)S(1)} %bitcast.120), channel_id=1, source_target_pairs={{0,2},{2,0},{4,6},{6,4},{8,10},{10,8},{12,14},{14,12},{16,18},{18,... | collective-permute-start | bytes 1990664 | tf_op jit(solution)/shard_map/ppermute | solution.py:565
  60.2 16.8 %collective-permute-start.19 = (bf16[432,768]{1,0:T(8,128)(2,1)S(1)}, bf16[432,768]{1,0:T(8,128)(2,1)S(1)}, u32[]{:S(2)}, u32[]{:S(2)}) collective-permute-start(bf16[432,768]{1,0:T(8,128)(2,1)S(1)} %collective-permute-done.7.refs_1_), channel_id=1, source_target_pairs={{0,8},{2,10},{8,16},{10,18},{16,24},{18,26},{24,28},{26,30},{28,20... | collective-permute-start | bytes 1990664 | tf_op jit(solution)/shard_map/ppermute | solution.py:554
  62.3 37.9 %collective-permute-start.25 = (bf16[432,768]{1,0:T(8,128)(2,1)S(1)}, bf16[432,768]{1,0:T(8,128)(2,1)S(1)}, u32[]{:S(2)}, u32[]{:S(2)}) collective-permute-start(bf16[432,768]{1,0:T(8,128)(2,1)S(1)} %collective-permute-done.7.refs_1_), channel_id=1, source_target_pairs={{0,2},{2,0},{4,6},{6,4},{8,10},{10,8},{12,14},{14,12},{16,18},{18,... | collective-permute-start | bytes 1990664 | tf_op jit(solution)/shard_map/ppermute | solution.py:565
  62.4 17.6 %collective-permute-start.20 = (bf16[432,768]{1,0:T(8,128)(2,1)}, bf16[432,768]{1,0:T(8,128)(2,1)}, u32[]{:S(2)}, u32[]{:S(2)}) collective-permute-start(bf16[432,768]{1,0:T(8,128)(2,1)} %collective-permute-done.8.refs_5_), channel_id=1, source_target_pairs={{0,4},{2,6},{8,0},{10,2},{16,8},{18,10},{24,16},{26,18},{28,24},{3... | collective-permute-start | bytes 1990664 | tf_op jit(solution)/shard_map/ppermute | solution.py:556
  62.6 37.7 %collective-permute-start.29 = (bf16[432,768]{1,0:T(8,128)(2,1)}, bf16[432,768]{1,0:T(8,128)(2,1)}, u32[]{:S(2)}, u32[]{:S(2)}) collective-permute-start(bf16[432,768]{1,0:T(8,128)(2,1)} %collective-permute-done.8.refs_5_), channel_id=1, source_target_pairs={{0,2},{2,0},{4,6},{6,4},{8,10},{10,8},{12,14},{14,12},{16,18},{18,... | collective-permute-start | bytes 1990664 | tf_op jit(solution)/shard_map/ppermute | solution.py:565
  81.4 16.6 %collective-permute-start.22 = (bf16[432,768]{1,0:T(8,128)(2,1)}, bf16[432,768]{1,0:T(8,128)(2,1)}, u32[]{:S(2)}, u32[]{:S(2)}) collective-permute-start(bf16[432,768]{1,0:T(8,128)(2,1)} %collective-permute-done.20.refs_6_), channel_id=1, source_target_pairs={{0,4},{2,6},{8,0},{10,2},{16,8},{18,10},{24,16},{26,18},{28,24},{3... | collective-permute-start | bytes 1990664 | tf_op jit(solution)/shard_map/ppermute | solution.py:556
  177.2 32.2 %collective-permute-start.35 = (bf16[6,432,768]{2,1,0:T(8,128)(2,1)}, bf16[6,432,768]{2,1,0:T(8,128)(2,1)S(1)}, u32[]{:S(2)}, u32[]{:S(2)}) collective-permute-start(bf16[6,432,768]{2,1,0:T(8,128)(2,1)} %get-tuple-element.158), channel_id=1, source_target_pairs={{0,2},{2,0},{4,6},{6,4},{8,10},{10,8},{12,14},{14,12},{16,18},{18,... | collective-permute-start | bytes 11943944 | tf_op jit(solution)/shard_map/ppermute | solution.py:596
  177.8 31.6 %collective-permute-start.36 = (bf16[512,768]{1,0:T(8,128)(2,1)}, bf16[512,768]{1,0:T(8,128)(2,1)}, u32[]{:S(2)}, u32[]{:S(2)}) collective-permute-start(bf16[512,768]{1,0:T(8,128)(2,1)} %get-tuple-element.159), channel_id=1, source_target_pairs={{0,1},{1,0},{2,3},{3,2},{4,5},{5,4},{6,7},{7,6},{8,9},{9,8},{10,11... | collective-permute-start | bytes 2359304 | tf_op jit(solution)/shard_map/ppermute | solution.py:631
  189.0 20.4 %collective-permute-start.33 = (bf16[432,768]{1,0:T(8,128)(2,1)}, bf16[432,768]{1,0:T(8,128)(2,1)}, u32[]{:S(2)}, u32[]{:S(2)}) collective-permute-start(bf16[432,768]{1,0:T(8,128)(2,1)} %get-tuple-element.148), channel_id=1, source_target_pairs={{0,8},{2,10},{8,16},{10,18},{16,24},{18,26},{24,28},{26,30},{28,20... | collective-permute-start | bytes 1990664 | tf_op jit(solution)/shard_map/ppermute | solution.py:610
  190.7 18.8 %collective-permute-start.34 = (bf16[432,768]{1,0:T(8,128)(2,1)}, bf16[432,768]{1,0:T(8,128)(2,1)}, u32[]{:S(2)}, u32[]{:S(2)}) collective-permute-start(bf16[432,768]{1,0:T(8,128)(2,1)} %get-tuple-element.149), channel_id=1, source_target_pairs={{0,4},{2,6},{8,0},{10,2},{16,8},{18,10},{24,16},{26,18},{28,24},{3... | collective-permute-start | bytes 1990664 | tf_op jit(solution)/shard_map/ppermute | solution.py:612
  214.2 21.3 %collective-permute-start.37 = (bf16[432,768]{1,0:T(8,128)(2,1)}, bf16[432,768]{1,0:T(8,128)(2,1)}, u32[]{:S(2)}, u32[]{:S(2)}) collective-permute-start(bf16[432,768]{1,0:T(8,128)(2,1)} %get-tuple-element.168), channel_id=1, source_target_pairs={{0,8},{2,10},{8,16},{10,18},{16,24},{18,26},{24,28},{26,30},{28,20... | collective-permute-start | bytes 1990664 | tf_op jit(solution)/shard_map/ppermute | solution.py:610
  215.9 19.7 %collective-permute-start.38 = (bf16[432,768]{1,0:T(8,128)(2,1)}, bf16[432,768]{1,0:T(8,128)(2,1)}, u32[]{:S(2)}, u32[]{:S(2)}) collective-permute-start(bf16[432,768]{1,0:T(8,128)(2,1)} %get-tuple-element.169), channel_id=1, source_target_pairs={{0,4},{2,6},{8,0},{10,2},{16,8},{18,10},{24,16},{26,18},{28,24},{3... | collective-permute-start | bytes 1990664 | tf_op jit(solution)/shard_map/ppermute | solution.py:612
  238.8 24.9 %collective-permute-start.39 = (bf16[432,768]{1,0:T(8,128)(2,1)}, bf16[432,768]{1,0:T(8,128)(2,1)}, u32[]{:S(2)}, u32[]{:S(2)}) collective-permute-start(bf16[432,768]{1,0:T(8,128)(2,1)} %get-tuple-element.186), channel_id=1, source_target_pairs={{0,8},{2,10},{8,16},{10,18},{16,24},{18,26},{24,28},{26,30},{28,20... | collective-permute-start | bytes 1990664 | tf_op jit(solution)/shard_map/ppermute | solution.py:610
  240.5 23.2 %collective-permute-start.40 = (bf16[432,768]{1,0:T(8,128)(2,1)}, bf16[432,768]{1,0:T(8,128)(2,1)S(1)}, u32[]{:S(2)}, u32[]{:S(2)}) collective-permute-start(bf16[432,768]{1,0:T(8,128)(2,1)} %get-tuple-element.187), channel_id=1, source_target_pairs={{0,4},{2,6},{8,0},{10,2},{16,8},{18,10},{24,16},{26,18},{28,24},{3... | collective-permute-start | bytes 1990664 | tf_op jit(solution)/shard_map/ppermute | solution.py:612
  264.6 24.5 %collective-permute-start.42 = (bf16[6,160,768]{2,1,0:T(8,128)(2,1)}, bf16[6,160,768]{2,1,0:T(8,128)(2,1)S(1)}, u32[]{:S(2)}, u32[]{:S(2)}) collective-permute-start(bf16[6,160,768]{2,1,0:T(8,128)(2,1)} %get-tuple-element.209), channel_id=1, source_target_pairs={{0,2},{2,0},{4,6},{6,4},{8,10},{10,8},{12,14},{14,12},{16,18},{18,... | collective-permute-start | bytes 4423688 | tf_op jit(solution)/shard_map/ppermute | solution.py:596
  266.9 24.4 %collective-permute-start.52 = (bf16[432,768]{1,0:T(8,128)(2,1)S(1)}, bf16[432,768]{1,0:T(8,128)(2,1)S(1)}, u32[]{:S(2)}, u32[]{:S(2)}) collective-permute-start(bf16[432,768]{1,0:T(8,128)(2,1)S(1)} %fusion), channel_id=1, source_target_pairs={{0,8},{2,10},{8,16},{10,18},{16,24},{18,26},{24,28},{26,30},{28,20... | collective-permute-start | bytes 1990664 | tf_op jit(solution)/shard_map/ppermute | solution.py:610
  269.8 19.2 %collective-permute-start.44 = (bf16[160,768]{1,0:T(8,128)(2,1)S(1)}, bf16[160,768]{1,0:T(8,128)(2,1)S(1)}, u32[]{:S(2)}, u32[]{:S(2)}) collective-permute-start(bf16[160,768]{1,0:T(8,128)(2,1)S(1)} %get-tuple-element.211), channel_id=1, source_target_pairs={{0,8},{2,10},{8,16},{10,18},{16,24},{18,26},{24,28},{26,30},{28,20... | collective-permute-start | bytes 737288 | tf_op jit(solution)/shard_map/ppermute | solution.py:610
  271.5 17.6 %collective-permute-start.45 = (bf16[160,768]{1,0:T(8,128)(2,1)S(1)}, bf16[160,768]{1,0:T(8,128)(2,1)S(1)}, u32[]{:S(2)}, u32[]{:S(2)}) collective-permute-start(bf16[160,768]{1,0:T(8,128)(2,1)S(1)} %get-tuple-element.212), channel_id=1, source_target_pairs={{0,4},{2,6},{8,0},{10,2},{16,8},{18,10},{24,16},{26,18},{28,24},{3... | collective-permute-start | bytes 737288 | tf_op jit(solution)/shard_map/ppermute | solution.py:612
  274.5 24.9 %collective-permute-start.41 = (bf16[512,768]{1,0:T(8,128)(2,1)S(1)}, bf16[512,768]{1,0:T(8,128)(2,1)S(1)}, u32[]{:S(2)}, u32[]{:S(2)}) collective-permute-start(bf16[512,768]{1,0:T(8,128)(2,1)S(1)} %copy-done.21), channel_id=1, source_target_pairs={{0,1},{1,0},{2,3},{3,2},{4,5},{5,4},{6,7},{7,6},{8,9},{9,8},{10,11... | collective-permute-start | bytes 2359304 | tf_op jit(solution)/shard_map/ppermute | solution.py:631
  (73 other events, 616.3 us)
